TPU v7x, 32 devices: a whole 2x2x4 slice. The times are simulated.
32 devices in a mesh: section: 4 (over z), dp: 8 (over y, x, core).
Axes of the slice: x: 2, y: 2, z: 4, core: 2. Of those that a mesh axis runs over, the one named last changes fastest.
Arguments:
- x_in: bfloat16 [8, 4, 128, 768], P('dp'), may hold values from -8 to 8
- cotangent: bfloat16 [8, 4, 128, 768], P('dp'), may hold values from -0.15625 to 0.15625
- w_in: bfloat16 [4, 768, 3072], P('section'), may hold values from -0.21875 to 0.21875
- w_out: bfloat16 [4, 768, 3072], P('section'), may hold values from -0.109375 to 0.109375
- gain: bfloat16 [4, 768], P('section'), may hold values from 0.099609375 to 1.8984375
- drop_mask: int32 [8, 4, 1, 4], P('dp'), may hold values 0 or 1
Outputs:
- grad_in: float32 [4, 768, 3072], P('section', 'dp')
- grad_out: float32 [4, 768, 3072], P('section', 'dp')
- grad_gain: float32 [4, 768], P('section', 'dp')
All inputs are finite; a program needn't handle non-finite values. No bound on the sum of `drop_mask` on one device may be relied on, other than what follows from the above.
Results may differ from a plain program's by a relative error of at most 0.035.
Values may be sent and summed in bfloat16 or wider, within the bound.
A program may use at most 256 MiB of HBM per device.

v0:
```python
import jax
import jax.numpy as jnp
from jax import lax
from jax.sharding import PartitionSpec as P

EPSILON = 1e-05
ROOT_HALF = 0.7071067811865476
DENSITY_SCALE = 0.3989422804014327


def shifted(block, axis, distance):
    devices = range(lax.axis_size(axis))
    route = [(i - distance, i) for i in devices if i - distance in devices]
    return lax.ppermute(block, axis, route)


def as_sent(shard):

    def short(part):
        return part.astype(jnp.bfloat16) if part.dtype == jnp.float32 else part

    return jax.tree.map(short, shard)


def gelu_exact(hidden):
    return 0.5 * hidden * (1.0 + lax.erf(hidden * ROOT_HALF))


def gelu_slope(hidden):
    return (
        0.5 * (1.0 + lax.erf(hidden * ROOT_HALF))
        + hidden * jnp.exp(-0.5 * hidden * hidden) * DENSITY_SCALE
    )


def block_forward(inputs, keep_rows, gain_row, w_first, w_second):
    as_float = inputs.astype(jnp.float32)
    inv_rms = lax.rsqrt(jnp.mean(as_float * as_float, axis=-1, keepdims=True) + EPSILON)
    normed = (as_float * inv_rms * gain_row.astype(jnp.float32)).astype(jnp.bfloat16)
    hidden = jnp.dot(normed, w_first, preferred_element_type=jnp.float32)
    active = gelu_exact(hidden).astype(jnp.bfloat16)
    branch = lax.dot_general(
        active, w_second, (((1,), (1,)), ((), ())), preferred_element_type=jnp.float32
    )
    outputs = (as_float + keep_rows[:, None] * branch).astype(jnp.bfloat16)
    return (outputs, normed, hidden, active, inv_rms)


def block_backward(
    upstream, inputs, keep_rows, gain_row, w_first, w_second, normed, hidden, active, inv_rms
):
    up_float = upstream.astype(jnp.float32)
    gated = (keep_rows[:, None] * up_float).astype(jnp.bfloat16)
    grad_second = lax.dot_general(
        gated, active, (((0,), (0,)), ((), ())), preferred_element_type=jnp.float32
    )
    grad_active = jnp.dot(gated, w_second, preferred_element_type=jnp.float32)
    grad_hidden = (grad_active * gelu_slope(hidden)).astype(jnp.bfloat16)
    grad_first = lax.dot_general(
        normed, grad_hidden, (((0,), (0,)), ((), ())), preferred_element_type=jnp.float32
    )
    grad_normed = lax.dot_general(
        grad_hidden, w_first, (((1,), (1,)), ((), ())), preferred_element_type=jnp.float32
    )
    as_float = inputs.astype(jnp.float32)
    grad_gain = jnp.sum(grad_normed * as_float * inv_rms, axis=0)
    scaled_grad = grad_normed * gain_row.astype(jnp.float32)
    centre = jnp.mean(scaled_grad * as_float, axis=-1, keepdims=True)
    grad_inputs = up_float + inv_rms * (scaled_grad - as_float * inv_rms * inv_rms * centre)
    return (grad_inputs.astype(jnp.bfloat16), grad_first, grad_second, grad_gain)


def spare_forward(operand, hidden_width):
    count_rows = operand.shape[0]
    return (
        operand,
        jnp.zeros_like(operand),
        jnp.zeros((count_rows, hidden_width), jnp.float32),
        jnp.zeros((count_rows, hidden_width), jnp.bfloat16),
        jnp.zeros((count_rows, 1), jnp.float32),
    )


def add_terms(totals, term_parts):
    return tuple((total + term for total, term in zip(totals, term_parts)))


def run_forward(block_in, sample_keep, weights, seq_len):
    w_first, w_second, gain_row = weights
    keep_rows = jnp.repeat(sample_keep, seq_len)
    return block_forward(block_in, keep_rows, gain_row, w_first, w_second)


def run_backward(upstream, saved_parts, sample_keep, weights, seq_len, totals):
    w_first, w_second, gain_row = weights
    keep_rows = jnp.repeat(sample_keep, seq_len)
    found = block_backward(
        upstream,
        saved_parts[0],
        keep_rows,
        gain_row,
        w_first,
        w_second,
        saved_parts[1],
        saved_parts[2],
        saved_parts[3],
        saved_parts[4],
    )
    return (found[0], add_terms(totals, found[1:]))


def send_higher(operand):
    return shifted(operand, "section", 1)


def send_lower(operand):
    return jax.tree.map(
        lambda part, own: part.astype(own.dtype), shifted(as_sent(operand), "section", -1), operand
    )


def store_slot(buffer, update, slot_index, active_now):
    previous = lax.dynamic_index_in_dim(buffer, slot_index, 0, keepdims=False)
    chosen = jnp.where(active_now, update, previous)
    return lax.dynamic_update_index_in_dim(buffer, chosen, slot_index, 0)


def per_device(x_in, cotangent, w_in, w_out, gain, drop_mask):
    sections = lax.axis_size("section")
    section_index = lax.axis_index("section")
    inputs = x_in[0]
    cot_rows = cotangent[0]
    drop_marks = drop_mask[0].astype(jnp.float32)
    micro_count = inputs.shape[0]
    row_count = inputs.shape[1]
    model_width = inputs.shape[2]
    hidden_width = w_in.shape[2]
    samples = drop_marks.shape[1]
    seq_len = row_count // samples
    half_count = micro_count // 2
    own_weights = (w_in[0], w_out[0], gain[0])
    streams = [(0, micro_count, 1, section_index, own_weights, -1)]

    def sample_marks(layer_index):
        select = (jnp.arange(drop_marks.shape[2]) == layer_index).astype(jnp.float32)
        return jnp.sum(drop_marks * select, axis=-1)

    keep_table = [sample_marks(stream[3]) for stream in streams]
    stream = streams[0]
    count = stream[1]
    stores = [
        (
            jnp.zeros((count, row_count, model_width), jnp.bfloat16),
            jnp.zeros((count, row_count, model_width), jnp.bfloat16),
            jnp.zeros((count, row_count, hidden_width), jnp.float32),
            jnp.zeros((count, row_count, hidden_width), jnp.bfloat16),
            jnp.zeros((count, row_count, 1), jnp.float32),
        )
    ]
    ticks = max((stream[1] for stream in streams)) + sections - 1
    incoming = [jnp.zeros((row_count, model_width), jnp.bfloat16) for stream in streams]
    for moment in range(ticks):
        outgoing = []
        for number, stream in enumerate(streams):
            start, count, direction, position, weights, half_mode = stream
            offset = moment - position
            active_now = jnp.logical_and(offset >= 0, offset < count)
            slot_index = jnp.clip(offset, 0, count - 1)
            entry_rows = lax.dynamic_index_in_dim(inputs, start + slot_index, 0, keepdims=False)
            block_in = jnp.where(position == 0, entry_rows, incoming[number])
            sample_keep = lax.dynamic_index_in_dim(
                keep_table[number], slot_index, 0, keepdims=False
            )
            result = lax.cond(
                active_now,
                lambda operand: run_forward(operand, sample_keep, weights, seq_len),
                lambda operand: spare_forward(operand, hidden_width),
                block_in,
            )
            saved_parts = (block_in,) + tuple(result[1:])
            stores[number] = tuple(
                (
                    store_slot(buffer, update, slot_index, active_now)
                    for buffer, update in zip(stores[number], saved_parts)
                )
            )
            outgoing.append(result[0])
        if moment + 1 < ticks:
            for number, stream in enumerate(streams):
                incoming[number] = send_higher(outgoing[number])
    zero_terms = (
        jnp.zeros((model_width, hidden_width), jnp.float32),
        jnp.zeros((model_width, hidden_width), jnp.float32),
        jnp.zeros((model_width,), jnp.float32),
    )
    stream = streams[0]
    accums = [(zero_terms, zero_terms)]
    incoming = [jnp.zeros((row_count, model_width), jnp.bfloat16) for stream in streams]
    for moment in range(ticks):
        outgoing = []
        for number, stream in enumerate(streams):
            start, count, direction, position, weights, half_mode = stream
            offset = moment - (sections - 1 - position)
            active_now = jnp.logical_and(offset >= 0, offset < count)
            slot_index = jnp.clip(offset, 0, count - 1)
            entry_rows = lax.dynamic_index_in_dim(cot_rows, start + slot_index, 0, keepdims=False)
            upstream = jnp.where(position == sections - 1, entry_rows, incoming[number])
            saved_parts = tuple(
                (
                    lax.dynamic_index_in_dim(buffer, slot_index, 0, keepdims=False)
                    for buffer in stores[number]
                )
            )
            sample_keep = lax.dynamic_index_in_dim(
                keep_table[number], slot_index, 0, keepdims=False
            )
            local_half = (start + slot_index >= half_count).astype(jnp.int32)
            branch_index = jnp.where(active_now, 1 + local_half, 0)

            def make_branch(
                which, saved_parts=saved_parts, sample_keep=sample_keep, weights=weights
            ):

                def branch(operand):
                    rows_now, sums_all = operand
                    flow_rows, updated = run_backward(
                        rows_now, saved_parts, sample_keep, weights, seq_len, sums_all[which]
                    )
                    renewed = list(sums_all)
                    renewed[which] = updated
                    return (flow_rows, tuple(renewed))

                return branch

            branches = [lambda operand: operand] + [
                make_branch(which) for which in range(len(accums[number]))
            ]
            flow_rows, accums[number] = lax.switch(
                branch_index, branches, (upstream, accums[number])
            )
            outgoing.append(flow_rows)
        if moment + 1 < ticks:
            for number, stream in enumerate(streams):
                incoming[number] = send_lower(outgoing[number])
    lower_halves = tuple((term.astype(jnp.bfloat16) for term in accums[0][0]))
    upper_halves = tuple((term.astype(jnp.bfloat16) for term in accums[-1][-1]))
    parts = tuple(
        (
            (first.astype(jnp.float32) + second.astype(jnp.float32))
            .astype(jnp.bfloat16)
            .astype(jnp.float32)
            for first, second in zip(lower_halves, upper_halves)
        )
    )
    reduced = (
        lax.psum_scatter(
            parts[0].astype(jnp.bfloat16), "dp", scatter_dimension=0, tiled=True
        ).astype(jnp.float32),
        lax.psum_scatter(
            parts[1].astype(jnp.bfloat16), "dp", scatter_dimension=0, tiled=True
        ).astype(jnp.float32),
        lax.psum_scatter(
            parts[2].astype(jnp.bfloat16), "dp", scatter_dimension=0, tiled=True
        ).astype(jnp.float32),
    )
    return (reduced[0][None], reduced[1][None], reduced[2][None])


def solution(mesh):
    placed = (
        P("dp", None, None, None),
        P("dp", None, None, None),
        P("section", None, None),
        P("section", None, None),
        P("section", None),
        P("dp", None, None, None),
    )
    return jax.shard_map(
        per_device,
        mesh=mesh,
        in_specs=placed,
        out_specs=(P("section", "dp", None), P("section", "dp", None), P("section", "dp")),
        check_vma=False,
    )
```

profile of v0, /device:TPU:0, one launch (start us, length us, event | category | flops | bytes accessed | tf_op | source)
XLA Modules:
  0.0 634.2 jit_solution(15972291746534953822)
XLA Ops:
  9.7 9.4 %conditional.14 = (bf16[128,768]{1,0:T(8,128)(2,1)S(1)}, bf16[128,768]{1,0:T(8,128)(2,1)S(1)}, f32[128,3072]{1,0:T(8,128)}, bf16[128,3072]{1,0:T(8,128)(2,1)}, f32[128,1]{0,1:T(1,128)S(1)}) conditional(s32[]{:T(128)} %convert_element_type.496, bf16[128,768]{1,0:T(8,128)(2,1)S(1)} %fusion.270, (bf16[128,768]{1,0:T(8,128)(2,1)S(1)}, f32[4]{0:T(128)S(1)}, ...), branch_computations={%region_1.2_spmd, %region_2.4_spmd} | conditional | flops 1211007872 | bytes 34220172 | solution.py:174
  37.6 8.8 %conditional.15 = (bf16[128,768]{1,0:T(8,128)(2,1)S(1)}, bf16[128,768]{1,0:T(8,128)(2,1)S(1)}, f32[128,3072]{1,0:T(8,128)S(1)}, bf16[128,3072]{1,0:T(8,128)(2,1)}, f32[128,1]{0,1:T(1,128)S(1)}) conditional(s32[]{:T(128)} %convert_element_type.500, bf16[128,768]{1,0:T(8,128)(2,1)S(1)} %get-tuple-element.1520, (bf16[128,768]{1,0:T(8,128)(2,1)S(1)}, ...), branch_computations={%region_4.5_spmd, %region_5.7_spmd} | conditional | flops 1211007872 | bytes 34220172 | solution.py:174
  60.9 6.4 %conditional.16 = (bf16[128,768]{1,0:T(8,128)(2,1)S(1)}, bf16[128,768]{1,0:T(8,128)(2,1)S(1)}, f32[128,3072]{1,0:T(8,128)S(1)}, bf16[128,3072]{1,0:T(8,128)(2,1)}, f32[128,1]{0,1:T(1,128)S(1)}) conditional(s32[]{:T(128)} %convert_element_type.501, bf16[128,768]{1,0:T(8,128)(2,1)S(1)} %get-tuple-element.1518, (bf16[128,768]{1,0:T(8,128)(2,1)S(1)}, ...), branch_computations={%region_7.8_spmd, %region_8.10_spmd} | conditional | flops 1211007872 | bytes 15345776 | solution.py:174
  82.0 6.4 %conditional.17 = (bf16[128,768]{1,0:T(8,128)(2,1)S(1)}, bf16[128,768]{1,0:T(8,128)(2,1)S(1)}, f32[128,3072]{1,0:T(8,128)S(1)}, bf16[128,3072]{1,0:T(8,128)(2,1)}, f32[128,1]{0,1:T(1,128)S(1)}) conditional(s32[]{:T(128)} %convert_element_type.502, bf16[128,768]{1,0:T(8,128)(2,1)S(1)} %get-tuple-element.1516, (bf16[128,768]{1,0:T(8,128)(2,1)S(1)}, ...), branch_computations={%region_10.11_spmd, %region_11.13_spmd} | conditional | flops 1211007872 | bytes 34220172 | solution.py:174
  137.4 13.2 %conditional.20 = (bf16[128,768]{1,0:T(8,128)(2,1)}, f32[128,3072]{1,0:T(8,128)S(1)}, bf16[128,3072]{1,0:T(8,128)(2,1)S(1)}, f32[128,1]{0,1:T(1,128)S(1)}) conditional(s32[]{:T(128)} %convert_element_type.505, () %tuple.156, (bf16[128,768]{1,0:T(8,128)(2,1)S(1)}, bf16[768]{0:T(1024)(128)(2,1)S(1)}, bf16[768,3072]{1,0:T(8,128)(2,1)S(1)}) %tuple.346), branch_computations={%region_19.20_spmd, %region_20.22_spmd} | conditional | flops 606634880 | bytes 7874592 | solution.py:174
  164.9 20.0 %conditional.21 = (bf16[128,768]{1,0:T(8,128)(2,1)}, f32[768,3072]{1,0:T(8,128)}, f32[768,3072]{1,0:T(8,128)}, f32[768]{0:T(1024)S(1)}, f32[768,3072]{1,0:T(8,12...) conditional(s32[]{:T(128)} %clamp.27, bf16[128,768]{1,0:T(8,128)(2,1)S(1)} %select_bitcast_fusion, ...), branch_computations={%region_22.23_spmd, %region_23.26_spmd, %region_26.29_spmd} | conditional | flops 2422112256 | bytes 57234568 | solution.py:238
  194.4 19.1 %conditional.22 = (bf16[128,768]{1,0:T(8,128)(2,1)}, f32[768,3072]{0,1:T(8,128)}, f32[768,3072]{1,0:T(8,128)}, f32[768]{0:T(1024)S(1)}, f32[768,3072]{1,0:T(8,12...) conditional(s32[]{:T(128)} %clamp.26, (bf16[128,768]{1,0:T(8,128)(2,1)S(1)}, ...), branch_computations={%region_29.30_spmd, %region_30.33_spmd, %region_33.36_spmd} | conditional | flops 2426831616 | bytes 130379416 | solution.py:238
  194.4 9.6 %copy.31 = f32[768,3072]{0,1:T(8,128)} copy(f32[768,3072]{1,0:T(8,128)} %get-tuple-element.1368) | data formatting | bytes 18874368 | tf_op jit(solution)/shard_map
  214.8 6.5 %collective-permute-done.7 = bf16[128,768]{1,0:T(8,128)(2,1)S(1)} collective-permute-done((bf16[128,768]{1,0:T(8,128)(2,1)}, bf16[128,768]{1,0:T(8,128)(2,1)S(1)}, u32[]{:S(2)}, u32[]{:S(2)}) %collective-permute-start.7) | collective-permute-done | bytes 196640 | tf_op jit(solution)/shard_map/ppermute | solution.py:14
  223.7 53.1 %collective-permute-done.8 = bf16[128,768]{1,0:T(8,128)(2,1)S(1)} collective-permute-done((bf16[128,768]{1,0:T(8,128)(2,1)S(1)}, bf16[128,768]{1,0:T(8,128)(2,1)S(1)}, u32[]{:S(2)}, u32[]{:S(2)}) %collective-permute-start.8) | collective-permute-done | bytes 196640 | tf_op jit(solution)/shard_map/ppermute | solution.py:14
  277.8 21.9 %conditional.24 = (bf16[128,768]{1,0:T(8,128)(2,1)S(1)}, f32[768,3072]{0,1:T(8,128)}, f32[768,3072]{1,0:T(8,128)}, f32[768]{0:T(1024)S(1)}, f32[768,3072]{1,0:T(...) conditional(s32[]{:T(128)} %clamp.24, (bf16[128,768]{1,0:T(8,128)(2,1)S(1)}, ...), branch_computations={%region_43.44_spmd, %region_44.47_spmd, %region_47.50_spmd} | conditional | flops 2426831616 | bytes 148465312 | solution.py:238
  287.4 12.0 %convolution_add_fusion.4 = f32[768,3072]{1,0:T(8,128)} fusion(f32[768,3072]{1,0:T(8,128)} %get-tuple-element.884, bf16[128,3072]{1,0:T(8,128)(2,1)S(1)} %get-tuple-element.885, bf16[128,768]{1,0:T(8,128)(2,1)S(1)} %get-tuple-element.874, f32[]{:T(128)} %bitcast.40), kind=kOutput, calls=%fused_computation.243 | convolution fusion | flops 606633984 | bytes 19857412 | tf_op jit(solution)/shard_map/cond/branch_1_fun/dot_general | solution.py:54
  301.1 6.3 collective-permute-done.9
  308.3 22.6 %conditional.25 = (bf16[128,768]{1,0:T(8,128)(2,1)S(1)}, f32[768,3072]{0,1:T(8,128)}, f32[768,3072]{1,0:T(8,128)}, f32[768]{0:T(1024)S(1)}, f32[768,3072]{1,0:T(...) conditional(s32[]{:T(128)} %clamp.23, (bf16[128,768]{1,0:T(8,128)(2,1)S(1)}, ...), branch_computations={%region_50.51_spmd, %region_51.54_spmd, %region_54.57_spmd} | conditional | flops 2426831616 | bytes 148467392 | solution.py:238
  318.9 12.0 %convolution_add_fusion.6 = f32[768,3072]{1,0:T(8,128)} fusion(f32[768,3072]{1,0:T(8,128)} %get-tuple-element.916, bf16[128,3072]{1,0:T(8,128)(2,1)S(1)} %get-tuple-element.917, bf16[128,768]{1,0:T(8,128)(2,1)S(1)} %get-tuple-element.906, f32[]{:T(128)} %bitcast.46), kind=kOutput, calls=%fused_computation.291 | convolution fusion | flops 606633984 | bytes 19857412 | tf_op jit(solution)/shard_map/cond/branch_1_fun/dot_general | solution.py:54
  332.2 71.6 %collective-permute-done.10 = bf16[128,768]{1,0:T(8,128)(2,1)S(1)} collective-permute-done((bf16[128,768]{1,0:T(8,128)(2,1)S(1)}, bf16[128,768]{1,0:T(8,128)(2,1)S(1)}, u32[]{:S(2)}, u32[]{:S(2)}) %collective-permute-start.10) | collective-permute-done | bytes 196640 | tf_op jit(solution)/shard_map/ppermute | solution.py:14
  404.8 45.2 %conditional.26 = (bf16[128,768]{1,0:T(8,128)(2,1)S(1)}, f32[768,3072]{0,1:T(8,128)}, f32[768,3072]{1,0:T(8,128)}, f32[768]{0:T(1024)S(1)}, f32[768,3072]{1,0:T(...) conditional(s32[]{:T(128)} %clamp.22, (bf16[128,768]{1,0:T(8,128)(2,1)S(1)}, ...), branch_computations={%region_57.58_spmd, %region_58.61_spmd, %region_61.64_spmd} | conditional | flops 2426831616 | bytes 148465312 | solution.py:238
  412.4 9.7 %copy.38 = f32[768,3072]{0,1:T(8,128)} copy(f32[768,3072]{1,0:T(8,128)} %get-tuple-element.1463) | data formatting | bytes 18874368 | tf_op jit(solution)/shard_map
  422.1 8.8 %bitcast_add_fusion.9 = f32[768,3072]{0,1:T(8,128)} fusion(f32[768,3072]{0,1:T(8,128)} %copy.38, bf16[128,3072]{1,0:T(8,128)(2,1)S(1)} %fusion.240, bf16[128,768]{1,0:T(8,128)(2,1)S(1)} %get-tuple-element.966), kind=kOutput, calls=%fused_computation.362 | convolution fusion | flops 606339072 | bytes 19857408 | tf_op jit(solution)/shard_map/cond/branch_2_fun/dot_general | solution.py:59
  430.9 9.7 %copy.29 = f32[768,3072]{1,0:T(8,128)} copy(f32[768,3072]{0,1:T(8,128)} %bitcast_add_fusion.9) | data formatting | bytes 18874368 | tf_op jit(solution)/shard_map
  440.5 9.4 %convolution_add_fusion.9 = f32[768,3072]{1,0:T(8,128)} fusion(f32[768,3072]{1,0:T(8,128)} %get-tuple-element.967, bf16[128,3072]{1,0:T(8,128)(2,1)S(1)} %get-tuple-element.968, bf16[128,768]{1,0:T(8,128)(2,1)S(1)} %get-tuple-element.954, f32[]{:T(128)} %bitcast.55), kind=kOutput, calls=%fused_computation.363 | convolution fusion | flops 606633984 | bytes 19857412 | tf_op jit(solution)/shard_map/cond/branch_2_fun/dot_general | solution.py:54
  458.6 46.6 %conditional.27 = ((f32[768,3072]{0,1:T(8,128)}, f32[768,3072]{1,0:T(8,128)}, f32[768]{0:T(1024)S(1)}, f32[768,3072]{1,0:T(8,128)}, f32[768,3072]{1,0:T(8,128)}, /*index=5*/f32[768]{0:T(1024)S(1)})) conditional(s32[]{:T(128)} %clamp.21, (f32[768,3072]{0,1:T(8,128)}, f32[768,3072]{1,0:T(8,128)}, f32[768]{0:T(1024)S(1)}, ...), branch_computations={%region_64.65_spmd, %region_65.67_spmd, %region_67.69_spmd} | conditional | flops 2425552896 | bytes 142359264 | solution.py:238
  463.5 9.7 %copy.39 = f32[768,3072]{0,1:T(8,128)} copy(f32[768,3072]{1,0:T(8,128)} %get-tuple-element.1475) | data formatting | bytes 18874368 | tf_op jit(solution)/shard_map
  473.1 8.8 %bitcast_add_fusion.11 = f32[768,3072]{0,1:T(8,128)} fusion(f32[768,3072]{0,1:T(8,128)} %copy.39, bf16[128,3072]{1,0:T(8,128)(2,1)S(1)} %fusion.263, bf16[128,768]{1,0:T(8,128)(2,1)S(1)} %get-tuple-element.993), kind=kOutput, calls=%fused_computation.399 | convolution fusion | flops 606339072 | bytes 19857408 | tf_op jit(solution)/shard_map/cond/branch_2_fun/dot_general | solution.py:59
  481.9 9.7 %copy.30 = f32[768,3072]{1,0:T(8,128)} copy(f32[768,3072]{0,1:T(8,128)} %bitcast_add_fusion.11) | data formatting | bytes 18874368 | tf_op jit(solution)/shard_map
  495.6 9.3 %convolution_add_fusion.11 = f32[768,3072]{1,0:T(8,128)} fusion(f32[768,3072]{1,0:T(8,128)} %get-tuple-element.994, bf16[128,3072]{1,0:T(8,128)(2,1)S(1)} %get-tuple-element.995, bf16[128,768]{1,0:T(8,128)(2,1)S(1)} %get-tuple-element.990, f32[]{:T(128)} %bitcast.60), kind=kOutput, calls=%fused_computation.400 | convolution fusion | flops 606633984 | bytes 19857412 | tf_op jit(solution)/shard_map/cond/branch_2_fun/dot_general | solution.py:54
  505.2 10.1 %add_convert_fusion = bf16[768,3072]{1,0:T(8,128)(2,1)} fusion(f32[768,3072]{1,0:T(8,128)} %get-tuple-element.1164, f32[768,3072]{1,0:T(8,128)} %get-tuple-element.1163), kind=kLoop, calls=%fused_computation.412 | loop fusion | flops 14155776 | bytes 23592960 | tf_op jit(solution)/shard_map/convert_element_type | solution.py:250
  515.4 8.3 %copy.40 = bf16[768,3072]{1,0:T(8,128)(2,1)} copy(f32[768,3072]{0,1:T(8,128)} %get-tuple-element.1161) | data formatting | bytes 14155776 | tf_op jit(solution)/shard_map/cond | solution.py:238
  523.6 9.7 %add_convert_fusion.1 = bf16[768,3072]{1,0:T(8,128)(2,1)} fusion(f32[768,3072]{1,0:T(8,128)} %get-tuple-element.1162, bf16[768,3072]{1,0:T(8,128)(2,1)} %copy.40), kind=kLoop, calls=%fused_computation.413 | loop fusion | flops 11796480 | bytes 18874368 | tf_op jit(solution)/shard_map/convert_element_type | solution.py:250
  535.2 12.2 %all-reduce = bf16[768]{0:T(1024)(128)(2,1)S(1)} all-reduce(bf16[768]{0:T(1024)(128)(2,1)S(1)} %add_convert_fusion.2), channel_id=4, replica_groups=mesh['section'=4,'dp'=8] {'dp'}, use_global_device_ids=true, to_apply=%region_71.72.clone | all-reduce | flops 768 | bytes 3072
  548.1 19.0 %reduce-scatter.5.cloned.1.call-done = bf16[96,3072]{1,0:T(8,128)(2,1)} async-done(((bf16[768,3072]{1,0:T(8,128)(2,1)}), bf16[96,3072]{1,0:T(8,128)(2,1)}) %reduce-scatter.5.cloned.1.call-update) | async-done | bytes 589840 | tf_op jit(solution)/shard_map/reduce_scatter | solution.py:259
  569.2 55.6 %reduce-scatter.3.cloned.1.call-done = bf16[96,3072]{1,0:T(8,128)(2,1)} async-done(((bf16[768,3072]{1,0:T(8,128)(2,1)}), bf16[96,3072]{1,0:T(8,128)(2,1)}) %reduce-scatter.3.cloned.1.call-update) | async-done | bytes 589840 | tf_op jit(solution)/shard_map/reduce_scatter | solution.py:256
  (357 shorter events, 236.5 us)
Async XLA Ops:
  7.2 559.9 %reduce-scatter.5.cloned.1.call-start = ((), (), s32[]{:S(2)}) async-start(), calls=%async_computation.3 | async-start | bytes 5308416 | tf_op jit(solution)/shard_map/reduce_scatter | solution.py:259
  19.6 16.1 %collective-permute-start = (bf16[128,768]{1,0:T(8,128)(2,1)S(1)}, bf16[128,768]{1,0:T(8,128)(2,1)}, u32[]{:S(2)}, u32[]{:S(2)}) collective-permute-start(bf16[128,768]{1,0:T(8,128)(2,1)S(1)} %get-tuple-element.1086), channel_id=1, source_target_pairs={{0,8},{8,16},{16,24},{1,9},{9,17},{17,25},{2,10},{10,18},{18,26},{... | collective-permute-start | bytes 589832 | tf_op jit(solution)/shard_map/ppermute | solution.py:14
  46.4 12.8 %collective-permute-start.1 = (bf16[128,768]{1,0:T(8,128)(2,1)S(1)}, bf16[128,768]{1,0:T(8,128)(2,1)S(1)}, u32[]{:S(2)}, u32[]{:S(2)}) collective-permute-start(bf16[128,768]{1,0:T(8,128)(2,1)S(1)} %get-tuple-element.1088), channel_id=1, source_target_pairs={{0,8},{8,16},{16,24},{1,9},{9,17},{17,25},{2,10},{10,18},{18,26},{... | collective-permute-start | bytes 589832 | tf_op jit(solution)/shard_map/ppermute | solution.py:14
  49.4 11.4 %slice-start = ((s8[4718592]{0:T(1024)(128)(4,1)}), s8[4194304]{0:T(1024)(128)(4,1)S(1)}, s32[]{:S(2)}) async-start(s8[4718592]{0:T(1024)(128)(4,1)} %bitcast.537), calls=%async_computation.4 | async-start | bytes 8388608
  67.3 13.0 %collective-permute-start.2 = (bf16[128,768]{1,0:T(8,128)(2,1)S(1)}, bf16[128,768]{1,0:T(8,128)(2,1)S(1)}, u32[]{:S(2)}, u32[]{:S(2)}) collective-permute-start(bf16[128,768]{1,0:T(8,128)(2,1)S(1)} %get-tuple-element.1090), channel_id=1, source_target_pairs={{0,8},{8,16},{16,24},{1,9},{9,17},{17,25},{2,10},{10,18},{18,26},{... | collective-permute-start | bytes 589832 | tf_op jit(solution)/shard_map/ppermute | solution.py:14
  70.6 11.4 %slice-start.2 = ((s8[4718592]{0:T(1024)(128)(4,1)}), s8[4194304]{0:T(1024)(128)(4,1)S(1)}, s32[]{:S(2)}) async-start(s8[4718592]{0:T(1024)(128)(4,1)} %bitcast.540), calls=%async_computation.6 | async-start | bytes 8388608
  88.4 12.8 %collective-permute-start.3 = (bf16[128,768]{1,0:T(8,128)(2,1)S(1)}, bf16[128,768]{1,0:T(8,128)(2,1)S(1)}, u32[]{:S(2)}, u32[]{:S(2)}) collective-permute-start(bf16[128,768]{1,0:T(8,128)(2,1)S(1)} %get-tuple-element.1092), channel_id=1, source_target_pairs={{0,8},{8,16},{16,24},{1,9},{9,17},{17,25},{2,10},{10,18},{18,26},{... | collective-permute-start | bytes 589832 | tf_op jit(solution)/shard_map/ppermute | solution.py:14
  91.4 11.4 %slice-start.4 = ((s8[4718592]{0:T(1024)(128)(4,1)}), s8[4194304]{0:T(1024)(128)(4,1)S(1)}, s32[]{:S(2)}) async-start(s8[4718592]{0:T(1024)(128)(4,1)} %bitcast.543), calls=%async_computation.8 | async-start | bytes 8388608
  104.0 15.6 %collective-permute-start.4 = (bf16[128,768]{1,0:T(8,128)(2,1)S(1)}, bf16[128,768]{1,0:T(8,128)(2,1)S(1)}, u32[]{:S(2)}, u32[]{:S(2)}) collective-permute-start(bf16[128,768]{1,0:T(8,128)(2,1)S(1)} %get-tuple-element.1094), channel_id=1, source_target_pairs={{0,8},{8,16},{16,24},{1,9},{9,17},{17,25},{2,10},{10,18},{18,26},{... | collective-permute-start | bytes 589832 | tf_op jit(solution)/shard_map/ppermute | solution.py:14
  110.0 11.3 %slice-start.6 = ((s8[4718592]{0:T(1024)(128)(4,1)}), s8[4194304]{0:T(1024)(128)(4,1)S(1)}, s32[]{:S(2)}) async-start(s8[4718592]{0:T(1024)(128)(4,1)} %bitcast.546), calls=%async_computation.10 | async-start | bytes 8388608
  122.5 13.3 %collective-permute-start.5 = (bf16[128,768]{1,0:T(8,128)(2,1)S(1)}, bf16[128,768]{1,0:T(8,128)(2,1)S(1)}, u32[]{:S(2)}, u32[]{:S(2)}) collective-permute-start(bf16[128,768]{1,0:T(8,128)(2,1)S(1)} %get-tuple-element.1096), channel_id=1, source_target_pairs={{0,8},{8,16},{16,24},{1,9},{9,17},{17,25},{2,10},{10,18},{18,26},{... | collective-permute-start | bytes 589832 | tf_op jit(solution)/shard_map/ppermute | solution.py:14
  126.1 11.3 %slice-start.8 = ((s8[4718592]{0:T(1024)(128)(4,1)}), s8[4194304]{0:T(1024)(128)(4,1)S(1)}, s32[]{:S(2)}) async-start(s8[4718592]{0:T(1024)(128)(4,1)} %bitcast.549), calls=%async_computation.12 | async-start | bytes 8388608
  184.9 8.5 %collective-permute-start.6 = (bf16[128,768]{1,0:T(8,128)(2,1)}, bf16[128,768]{1,0:T(8,128)(2,1)S(1)}, u32[]{:S(2)}, u32[]{:S(2)}) collective-permute-start(bf16[128,768]{1,0:T(8,128)(2,1)} %get-tuple-element.1119), channel_id=1, source_target_pairs={{8,0},{16,8},{24,16},{9,1},{17,9},{25,17},{10,2},{18,10},{26,18},{... | collective-permute-start | bytes 589832 | tf_op jit(solution)/shard_map/ppermute | solution.py:14
  194.4 27.8 %copy-start.35 = (bf16[128,3072]{1,0:T(8,128)(2,1)S(1)}, bf16[128,3072]{1,0:T(8,128)(2,1)}, u32[]{:S(2)}) copy-start(bf16[128,3072]{1,0:T(8,128)(2,1)} %get-tuple-element.1571) | copy-start | bytes 2359300
  213.5 7.8 %collective-permute-start.7 = (bf16[128,768]{1,0:T(8,128)(2,1)}, bf16[128,768]{1,0:T(8,128)(2,1)S(1)}, u32[]{:S(2)}, u32[]{:S(2)}) collective-permute-start(bf16[128,768]{1,0:T(8,128)(2,1)} %get-tuple-element.1126), channel_id=1, source_target_pairs={{8,0},{16,8},{24,16},{9,1},{17,9},{25,17},{10,2},{18,10},{26,18},{... | collective-permute-start | bytes 589832 | tf_op jit(solution)/shard_map/ppermute | solution.py:14
  222.2 55.6 %copy-start.34 = (bf16[128,3072]{1,0:T(8,128)(2,1)S(1)}, bf16[128,3072]{1,0:T(8,128)(2,1)}, u32[]{:S(2)}) copy-start(bf16[128,3072]{1,0:T(8,128)(2,1)} %get-tuple-element.1570) | copy-start | bytes 2359300
  222.2 55.6 %copy-start.48 = (bf16[128,768]{1,0:T(8,128)(2,1)S(1)}, bf16[128,768]{1,0:T(8,128)(2,1)}, u32[]{:S(2)}) copy-start(bf16[128,768]{1,0:T(8,128)(2,1)} %get-tuple-element.1599) | copy-start | bytes 589828
  222.3 54.5 %collective-permute-start.8 = (bf16[128,768]{1,0:T(8,128)(2,1)S(1)}, bf16[128,768]{1,0:T(8,128)(2,1)S(1)}, u32[]{:S(2)}, u32[]{:S(2)}) collective-permute-start(bf16[128,768]{1,0:T(8,128)(2,1)S(1)} %get-tuple-element.1133), channel_id=1, source_target_pairs={{8,0},{16,8},{24,16},{9,1},{17,9},{25,17},{10,2},{18,10},{26,18},{... | collective-permute-start | bytes 589832 | tf_op jit(solution)/shard_map/ppermute | solution.py:14
  277.8 30.5 %copy-start.33 = (bf16[128,3072]{1,0:T(8,128)(2,1)S(1)}, bf16[128,3072]{1,0:T(8,128)(2,1)}, u32[]{:S(2)}) copy-start(bf16[128,3072]{1,0:T(8,128)(2,1)} %get-tuple-element.1569) | copy-start | bytes 2359300
  287.4 12.0 %copy-start.13 = (f32[768,3072]{0,1:T(8,128)}, f32[768,3072]{0,1:T(8,128)S(1)}, u32[]{:S(2)}) copy-start(f32[768,3072]{0,1:T(8,128)S(1)} %bitcast_add_fusion.4) | copy-start | bytes 28311556 | tf_op jit(solution)/shard_map/cond
  299.7 7.6 %collective-permute-start.9 = (bf16[128,768]{1,0:T(8,128)(2,1)S(1)}, bf16[128,768]{1,0:T(8,128)(2,1)S(1)}, u32[]{:S(2)}, u32[]{:S(2)}) collective-permute-start(bf16[128,768]{1,0:T(8,128)(2,1)S(1)} %get-tuple-element.1140), channel_id=1, source_target_pairs={{8,0},{16,8},{24,16},{9,1},{17,9},{25,17},{10,2},{18,10},{26,18},{... | collective-permute-start | bytes 589832 | tf_op jit(solution)/shard_map/ppermute | solution.py:14
  308.3 96.5 %copy-start.32 = (bf16[128,3072]{1,0:T(8,128)(2,1)S(1)}, bf16[128,3072]{1,0:T(8,128)(2,1)}, u32[]{:S(2)}) copy-start(bf16[128,3072]{1,0:T(8,128)(2,1)} %get-tuple-element.1568) | copy-start | bytes 2359300
  308.3 96.5 %copy-start.45 = (bf16[128,768]{1,0:T(8,128)(2,1)S(1)}, bf16[128,768]{1,0:T(8,128)(2,1)}, u32[]{:S(2)}) copy-start(bf16[128,768]{1,0:T(8,128)(2,1)} %get-tuple-element.1574) | copy-start | bytes 589828
  308.3 96.5 %copy-start.47 = (bf16[128,768]{1,0:T(8,128)(2,1)S(1)}, bf16[128,768]{1,0:T(8,128)(2,1)}, u32[]{:S(2)}) copy-start(bf16[128,768]{1,0:T(8,128)(2,1)} %get-tuple-element.1601) | copy-start | bytes 589828
  308.3 96.5 %copy-start.73 = (f32[128,1]{0,1:T(1,128)S(1)}, f32[128,1]{0,1:T(1,128)}, u32[]{:S(2)}) copy-start(f32[128,1]{0,1:T(1,128)} %get-tuple-element.1586) | copy-start | bytes 1540
  318.9 12.0 %copy-start.15 = (f32[768,3072]{0,1:T(8,128)}, f32[768,3072]{0,1:T(8,128)S(1)}, u32[]{:S(2)}) copy-start(f32[768,3072]{0,1:T(8,128)S(1)} %bitcast_add_fusion.6) | copy-start | bytes 28311556 | tf_op jit(solution)/shard_map/cond
  330.9 72.9 %collective-permute-start.10 = (bf16[128,768]{1,0:T(8,128)(2,1)S(1)}, bf16[128,768]{1,0:T(8,128)(2,1)S(1)}, u32[]{:S(2)}, u32[]{:S(2)}) collective-permute-start(bf16[128,768]{1,0:T(8,128)(2,1)S(1)} %get-tuple-element.1147), channel_id=1, source_target_pairs={{8,0},{16,8},{24,16},{9,1},{17,9},{25,17},{10,2},{18,10},{26,18},{... | collective-permute-start | bytes 589832 | tf_op jit(solution)/shard_map/ppermute | solution.py:14
  404.8 53.8 %copy-start.31 = (bf16[128,3072]{1,0:T(8,128)(2,1)S(1)}, bf16[128,3072]{1,0:T(8,128)(2,1)}, u32[]{:S(2)}) copy-start(bf16[128,3072]{1,0:T(8,128)(2,1)} %get-tuple-element.1567) | copy-start | bytes 2359300
  404.8 53.8 %copy-start.46 = (bf16[128,768]{1,0:T(8,128)(2,1)S(1)}, bf16[128,768]{1,0:T(8,128)(2,1)}, u32[]{:S(2)}) copy-start(bf16[128,768]{1,0:T(8,128)(2,1)} %get-tuple-element.1602) | copy-start | bytes 589828
  404.8 53.8 %copy-start.53 = (bf16[128,768]{1,0:T(8,128)(2,1)S(1)}, bf16[128,768]{1,0:T(8,128)(2,1)}, u32[]{:S(2)}) copy-start(bf16[128,768]{1,0:T(8,128)(2,1)} %get-tuple-element.1573) | copy-start | bytes 589828
  450.1 7.6 %collective-permute-start.11 = (bf16[128,768]{1,0:T(8,128)(2,1)S(1)}, bf16[128,768]{1,0:T(8,128)(2,1)S(1)}, u32[]{:S(2)}, u32[]{:S(2)}) collective-permute-start(bf16[128,768]{1,0:T(8,128)(2,1)S(1)} %get-tuple-element.1160), channel_id=1, source_target_pairs={{8,0},{16,8},{24,16},{9,1},{17,9},{25,17},{10,2},{18,10},{26,18},{... | collective-permute-start | bytes 589832 | tf_op jit(solution)/shard_map/ppermute | solution.py:14
  515.3 109.5 %reduce-scatter.3.cloned.1.call-start = ((), (), s32[]{:S(2)}) async-start(), calls=%async_computation.2 | async-start | bytes 5308416 | tf_op jit(solution)/shard_map/reduce_scatter | solution.py:256
  (61 other events, 278.7 us)
Sparse Core Ops, SparseCore 0:
  515.4 51.5 reduce-scatter.4
  570.9 53.8 reduce-scatter.2
where the time goes:
time: 644 us; the launch traced here: 634 us
  waiting for transfers between devices  221 us (34%)
  local copies, waits for them, and re-layouts  147 us (23%)
  matrix products  123 us (19%)
  other arithmetic  70.6 us (11%)
  loops' own time  23.1 us (4%)
  starting transfers between devices  20.8 us (3%)
  between operations  16.1 us (3%)
  blocking collectives  12.2 us (2%)
    ppermute x12, waiting for transfers between devices, shifted(): return lax.ppermute(block, axis, route)  147 us
    another operation x23, local copies, waits for them, and re-layouts  70.7 us
    reduce_scatter x1, waiting for transfers between devices, per_device(): lax.psum_scatter(parts[0].astype(jnp.bfloat16), 'dp', scatter_dimension=0...  55.6 us
    dot_general x4, matrix products, block_backward(): lax.dot_general(gated, active, (((0,), (0,)), ((), ())), preferred_elemen...  42.7 us
    dynamic_slice x24, local copies, waits for them, and re-layouts, store_slot(): previous = lax.dynamic_index_in_dim(buffer, slot_index, 0, keepdims=False)  38.6 us
    dynamic_update_slice x35, other arithmetic, store_slot(): return lax.dynamic_update_index_in_dim(buffer, chosen, slot_index, 0)  35.2 us
    dot_general x4, matrix products, block_backward(): lax.dot_general(normed, grad_hidden, (((0,), (0,)), ((), ())), preferred_...  21.3 us
    ppermute x12, starting transfers between devices, shifted(): return lax.ppermute(block, axis, route)  20.7 us
  transfers between devices with their start and end apart: 14, of which 8 were waited for; matrix products, arithmetic and copies ran while one was open for 15% of the time, Pallas kernels for 0%

commit v1 on v0

v1 whole, which is shorter than its diff:
```python
import functools

import jax
import jax.numpy as jnp
from jax import lax
from jax.experimental import pallas as pl
from jax.experimental.pallas import tpu as pltpu
from jax.sharding import PartitionSpec as P

EPSILON = 1e-05
ROOT_HALF = 0.7071067811865476
DENSITY_SCALE = 0.3989422804014327
MESH = pl.DeviceIdType.MESH

CHUNK_ROWS = 64
LAG = 2
HIDDEN_BLOCK = 512
TILE = 512
TRANSPOSED_RHS = (((1,), (1,)), ((), ()))


def largest_divisor(extent, limit, step):
    best = extent
    for size in range(step, min(extent, limit) + 1, step):
        if extent % size == 0:
            best = size
    return best


def position(block, order):
    place = 0
    for bit in order:
        place = 2 * place + ((block >> bit) & 1)
    return place


def kernel(
    dims, keep_ref, gain_ref, x_hbm, cot_hbm, w1_hbm, w2_hbm, grad_in_ref, grad_out_ref, grad_gain_ref,
    w1, w2, h_in, g_in, h_out, g_out, normed_all, gated_all, active_all, slope_all, hidden_grad_all,
    gain_sum, normed_t, gated_t, parts_a, parts_b, parts_g, *rest,
):
    sections, shards, chunk, chunks, seq_len, block, tile, tiles, steps = dims
    landed_a, landed_b, landed_g = rest[:steps], rest[steps : 2 * steps], rest[2 * steps : 3 * steps]
    (load_sem, h_send, h_recv, g_send, g_recv, a_send, a_recv, b_send, b_recv, e_send, e_recv) = rest[3 * steps :]
    width, hidden_width = w1.shape
    section = lax.axis_index("section")
    shard = lax.axis_index("dp")
    first, last = section == 0, section == sections - 1
    bits = [lax.rem(shard // (1 << b), 2) for b in range(steps)]
    partners = [shard + (1 - 2 * bits[b]) * (1 << b) for b in range(steps)]

    loads = [
        pltpu.make_async_copy(w1_hbm, w1, load_sem.at[0]),
        pltpu.make_async_copy(w2_hbm, w2, load_sem.at[1]),
    ]
    entry = pltpu.make_async_copy(x_hbm, h_in, load_sem.at[2])
    cotangents = pltpu.make_async_copy(cot_hbm, g_in, load_sem.at[3])
    pl.when(first)(entry.start)
    for load in loads:
        load.start()
    pl.when(last)(cotangents.start)

    barrier = pltpu.get_barrier_semaphore()

    def greet(where):
        pl.semaphore_signal(barrier, inc=1, device_id=where, device_id_type=MESH)

    pl.when(section > 0)(lambda: greet({"section": section - 1}))
    pl.when(section < sections - 1)(lambda: greet({"section": section + 1}))
    for partner in partners:
        greet({"dp": partner})
    neighbours = jnp.where(first, 0, 1) + jnp.where(last, 0, 1)
    pl.semaphore_wait(barrier, steps + neighbours)

    def h_copy(index):
        return pltpu.make_async_remote_copy(
            h_out.at[index], h_in.at[index], h_send.at[index], h_recv.at[index],
            device_id={"section": section + 1}, device_id_type=MESH,
        )

    def g_copy(index):
        return pltpu.make_async_remote_copy(
            g_out.at[index], g_in.at[index], g_send.at[index], g_recv.at[index],
            device_id={"section": section - 1}, device_id_type=MESH,
        )

    gain_row = gain_ref[...].astype(jnp.float32)
    gain_sum[...] = jnp.zeros_like(gain_sum)
    column_blocks = [slice(at, at + block) for at in range(0, hidden_width, block)]

    def keep_of(index):
        return keep_ref[(index * chunk) // seq_len, section].astype(jnp.float32)

    def forward(index):
        pl.when(section > 0)(lambda: h_copy(index).wait_recv())
        rows = pl.ds(pl.multiple_of(index * chunk, chunk), chunk)
        inputs = h_in[index].astype(jnp.float32)
        inv_rms = lax.rsqrt(jnp.mean(inputs * inputs, axis=-1, keepdims=True) + EPSILON)
        normed = (inputs * inv_rms * gain_row).astype(jnp.bfloat16)
        normed_all[rows, :] = normed
        branch = jnp.zeros((chunk, width), jnp.float32)
        for columns in column_blocks:
            hidden = jnp.dot(normed, w1[:, columns], preferred_element_type=jnp.float32)
            share = 0.5 * (1.0 + lax.erf(hidden * ROOT_HALF))
            active = (hidden * share).astype(jnp.bfloat16)
            active_all[rows, columns] = active
            slope_all[rows, columns] = share + hidden * jnp.exp(-0.5 * hidden * hidden) * DENSITY_SCALE
            branch += lax.dot_general(
                active, w2[:, columns], TRANSPOSED_RHS, preferred_element_type=jnp.float32
            )

        @pl.when(section < sections - 1)
        def _():
            h_out[index] = (inputs + keep_of(index) * branch).astype(jnp.bfloat16)
            h_copy(index).start()

    def backward(index):
        pl.when(section < sections - 1)(lambda: g_copy(index).wait_recv())
        rows = pl.ds(pl.multiple_of(index * chunk, chunk), chunk)
        inputs = h_in[index].astype(jnp.float32)
        inv_rms = lax.rsqrt(jnp.mean(inputs * inputs, axis=-1, keepdims=True) + EPSILON)
        upstream = g_in[index].astype(jnp.float32)
        gated = (keep_of(index) * upstream).astype(jnp.bfloat16)
        gated_all[rows, :] = gated
        grad_normed = jnp.zeros((chunk, width), jnp.float32)
        for columns in column_blocks:
            grad_active = jnp.dot(gated, w2[:, columns], preferred_element_type=jnp.float32)
            grad_hidden = (grad_active * slope_all[rows, columns]).astype(jnp.bfloat16)
            hidden_grad_all[rows, columns] = grad_hidden
            grad_normed += lax.dot_general(
                grad_hidden, w1[:, columns], TRANSPOSED_RHS, preferred_element_type=jnp.float32
            )
        gain_sum[0:1, :] += jnp.sum(grad_normed * inputs * inv_rms, axis=0, keepdims=True)

        @pl.when(section > 0)
        def _():
            scaled = grad_normed * gain_row
            centre = jnp.mean(scaled * inputs, axis=-1, keepdims=True)
            grads = upstream + inv_rms * (scaled - inputs * inv_rms * inv_rms * centre)
            g_out[index] = grads.astype(jnp.bfloat16)
            g_copy(index).start()

    pl.when(first)(entry.wait)
    for load in loads:
        load.wait()
    pl.when(last)(cotangents.wait)

    def tick(moment, carry):
        ahead = moment - LAG * section
        behind = moment - LAG * (2 * (sections - 1) - section)
        pl.when(jnp.logical_and(ahead >= 0, ahead < chunks))(lambda: forward(ahead))
        pl.when(jnp.logical_and(behind >= 0, behind < chunks))(lambda: backward(behind))
        return carry

    lax.fori_loop(0, chunks + 2 * LAG * (sections - 1), tick, 0)

    upwards = list(range(steps))
    downwards = upwards[:1] + upwards[:0:-1]
    block_rows = width // shards

    def halving(order, parts, landed, send_sem, recv_sem):
        def copy(at, step):
            half = shards >> (step + 1)
            bit = order[step]
            source = parts if step == 0 else landed[step - 1]
            return pltpu.make_async_remote_copy(
                source.at[at, pl.ds((1 - bits[bit]) * half, half)],
                landed[step].at[at],
                send_sem.at[at, step],
                recv_sem.at[at, step],
                device_id={"dp": partners[bit]},
                device_id_type=MESH,
            )

        def fill(at, value):
            for shard_at in range(shards):
                rows = value[shard_at * block_rows : (shard_at + 1) * block_rows]
                parts[at, position(shard_at, order)] = rows.astype(jnp.bfloat16)
            copy(at, 0).start()

        def advance(at, step, finish):
            copy(at, step).wait_recv()
            half = shards >> (step + 1)
            source = parts if step == 0 else landed[step - 1]
            own = source[at, pl.ds(bits[order[step]] * half, half)].astype(jnp.float32)
            total = own + landed[step][at].astype(jnp.float32)
            if step + 1 < steps:
                landed[step][at] = total.astype(jnp.bfloat16)
                copy(at, step + 1).start()
            else:
                finish(total[0])

        def close(at):
            for step in range(steps):
                copy(at, step).wait_send()

        return fill, advance, close

    fill_a, advance_a, close_a = halving(upwards, parts_a, landed_a, a_send, a_recv)
    fill_b, advance_b, close_b = halving(downwards, parts_b, landed_b, b_send, b_recv)
    fill_g, advance_g, close_g = halving(upwards, parts_g, landed_g, e_send, e_recv)

    normed_t[...] = normed_all[...].T
    gated_t[...] = gated_all[...].T
    gain_lanes = jnp.broadcast_to(gain_sum[0:1, :], (128, width)).T

    def finish_gain(total):
        grad_gain_ref[...] = jnp.transpose(total)[0:1, :]

    def turn(moment, carry):
        @pl.when(moment < tiles)
        def _():
            columns = pl.ds(pl.multiple_of(moment * tile, tile), tile)
            fill_a(
                moment,
                jnp.dot(normed_t[...], hidden_grad_all[:, columns], preferred_element_type=jnp.float32),
            )
            fill_b(
                moment, jnp.dot(gated_t[...], active_all[:, columns], preferred_element_type=jnp.float32)
            )

        for step in range(steps):
            at = moment - (step + 1)

            @pl.when(jnp.logical_and(at >= 0, at < tiles))
            def _(at=at, step=step):
                columns = pl.ds(pl.multiple_of(at * tile, tile), tile)

                def finish_a(total):
                    grad_in_ref[:, columns] = total

                def finish_b(total):
                    grad_out_ref[:, columns] = total

                advance_a(at, step, finish_a)
                advance_b(at, step, finish_b)

            pl.when(moment == step + 2)(lambda step=step: advance_g(0, step, finish_gain))
        return carry

    fill_g(0, gain_lanes)
    lax.fori_loop(0, max(tiles, 2) + steps, turn, 0)

    def close_chunk(index, carry):
        pl.when(section < sections - 1)(lambda: h_copy(index).wait_send())
        pl.when(section > 0)(lambda: g_copy(index).wait_send())
        return carry

    lax.fori_loop(0, chunks, close_chunk, 0)

    def close_tile(at, carry):
        close_a(at)
        close_b(at)
        return carry

    lax.fori_loop(0, tiles, close_tile, 0)
    close_g(0)


def per_device(x_in, cotangent, w_in, w_out, gain, drop_mask):
    sections = lax.axis_size("section")
    shards = lax.axis_size("dp")
    micro, micro_rows, width = x_in.shape[1:]
    hidden_width = w_in.shape[2]
    samples, layers = drop_mask.shape[2:]
    seq_len = micro_rows // samples
    rows = micro * micro_rows
    chunk = largest_divisor(seq_len, CHUNK_ROWS, 16)
    chunks = rows // chunk
    block = largest_divisor(hidden_width, HIDDEN_BLOCK, 128)
    tile = largest_divisor(hidden_width, TILE, 128)
    tiles = hidden_width // tile
    steps = shards.bit_length() - 1
    assert shards == 1 << steps and steps >= 1
    block_rows = width // shards
    dims = (sections, shards, chunk, chunks, seq_len, block, tile, tiles, steps)

    def landing(count, columns):
        return [
            pltpu.VMEM((count, shards >> (step + 1), block_rows, columns), jnp.bfloat16)
            for step in range(steps)
        ]

    chunk_shape = (chunks, chunk, width)
    any_spec = pl.BlockSpec(memory_space=pl.ANY)
    vmem_spec = pl.BlockSpec(memory_space=pltpu.VMEM)
    dma = pltpu.SemaphoreType.DMA
    macs = 6 * rows * width * hidden_width
    grad_in, grad_out, grad_gain = pl.pallas_call(
        functools.partial(kernel, dims),
        out_shape=(
            jax.ShapeDtypeStruct((block_rows, hidden_width), jnp.float32),
            jax.ShapeDtypeStruct((block_rows, hidden_width), jnp.float32),
            jax.ShapeDtypeStruct((1, block_rows), jnp.float32),
        ),
        in_specs=[pl.BlockSpec(memory_space=pltpu.SMEM), vmem_spec] + [any_spec] * 4,
        out_specs=(vmem_spec,) * 3,
        scratch_shapes=[
            pltpu.VMEM((width, hidden_width), jnp.bfloat16),
            pltpu.VMEM((width, hidden_width), jnp.bfloat16),
            *[pltpu.VMEM(chunk_shape, jnp.bfloat16) for _ in range(4)],
            pltpu.VMEM((rows, width), jnp.bfloat16),
            pltpu.VMEM((rows, width), jnp.bfloat16),
            pltpu.VMEM((rows, hidden_width), jnp.bfloat16),
            pltpu.VMEM((rows, hidden_width), jnp.float32),
            pltpu.VMEM((rows, hidden_width), jnp.bfloat16),
            pltpu.VMEM((8, width), jnp.float32),
            pltpu.VMEM((width, rows), jnp.bfloat16),
            pltpu.VMEM((width, rows), jnp.bfloat16),
            pltpu.VMEM((tiles, shards, block_rows, tile), jnp.bfloat16),
            pltpu.VMEM((tiles, shards, block_rows, tile), jnp.bfloat16),
            pltpu.VMEM((1, shards, block_rows, 128), jnp.bfloat16),
            *landing(tiles, tile),
            *landing(tiles, tile),
            *landing(1, 128),
            dma((4,)),
            *[dma((chunks,)) for _ in range(4)],
            *[dma((tiles, steps)) for _ in range(4)],
            *[dma((1, steps)) for _ in range(2)],
        ],
        compiler_params=pltpu.CompilerParams(
            collective_id=0, has_side_effects=True, vmem_limit_bytes=62 * 1024 * 1024
        ),
        cost_estimate=pl.CostEstimate(
            flops=2 * macs, bytes_accessed=8 * width * hidden_width, transcendentals=2 * rows * hidden_width
        ),
        name="window",
    )(
        drop_mask[0].reshape(micro * samples, layers),
        gain,
        x_in[0].reshape(chunk_shape),
        cotangent[0].reshape(chunk_shape),
        w_in[0],
        w_out[0],
    )
    return (grad_in[None], grad_out[None], grad_gain)


def solution(mesh):
    placed = (
        P("dp", None, None, None),
        P("dp", None, None, None),
        P("section", None, None),
        P("section", None, None),
        P("section", None),
        P("dp", None, None, None),
    )
    return jax.shard_map(
        per_device,
        mesh=mesh,
        in_specs=placed,
        out_specs=(P("section", "dp", None), P("section", "dp", None), P("section", "dp")),
        check_vma=False,
    )
```

time: 644 us -> 138 us (0.21); the launches traced: 634 us -> 138 us
  waiting for transfers between devices: 221 us -> 0 us
  local copies, waits for them, and re-layouts: 147 us -> 3.99 us
  Pallas kernels: 0 us -> 133 us
  matrix products: 123 us -> 0 us
  other arithmetic: 70.6 us -> 0 us
  loops' own time: 23.1 us -> 0 us
  starting transfers between devices: 20.8 us -> 0 us
  between operations: 16.1 us -> 0.65 us
  blocking collectives: 12.2 us -> 0 us
    ppermute x12 -> x0, waiting for transfers between devices: 147 us -> none  [shifted(): return lax.ppermute(block, axis, route)]
    pallas_call x0 -> x1, Pallas kernels: none -> 133 us  [per_device(): pl.pallas_call(functools.partial(kernel, dims), out_shape=(jax.ShapeDtype...]
    dot_general x24 -> x0, matrix products: 123 us -> none  [the longest x4 42.7 us: block_backward(): lax.dot_general(gated, active, (((0,), (0,)), ((), ())), preferred_elemen...]
    reduce_scatter x2 -> x0, waiting for transfers between devices: 74.6 us -> none  [the longest x1 55.6 us: per_device(): lax.psum_scatter(parts[0].astype(jnp.bfloat16), 'dp', scatter_dimension=0...]
    another operation x23 -> x0, local copies, waits for them, and re-layouts: 70.7 us -> none
    dynamic_slice x24 -> x0, local copies, waits for them, and re-layouts: 38.6 us -> none  [store_slot(): previous = lax.dynamic_index_in_dim(buffer, slot_index, 0, keepdims=False)]
    dynamic_update_slice x35 -> x0, other arithmetic: 35.2 us -> none  [store_slot(): return lax.dynamic_update_index_in_dim(buffer, chosen, slot_index, 0)]
    another operation x14 -> x0, loops' own time: 23.1 us -> none  [the longest x7 12.6 us: per_device(): lax.cond(active_now, lambda operand: run_forward(operand, sample_keep, we...]
  transfers between devices with their start and end apart: 14 -> 0, of which waited for: 8 -> 0; matrix products, arithmetic and copies ran while one was open for 15% -> 0% of each run, Pallas kernels for 0% -> 0%
where the time goes in v1:
time: 138 us
  Pallas kernels  133 us (96%)
  local copies, waits for them, and re-layouts  3.99 us (3%)
    pallas_call x1, Pallas kernels, per_device(): pl.pallas_call(functools.partial(kernel, dims), out_shape=(jax.ShapeDtype...  133 us
    unnamed x7, local copies, waits for them, and re-layouts  3.99 us

profile of v1, /device:TPU:0, one launch (start us, length us, event | category | flops | bytes accessed | tf_op | source)
XLA Modules:
  0.0 137.7 jit_solution(11206429783805264120)
XLA Ops:
  0.6 133.0 %window.1 = (f32[96,3072]{1,0:T(8,128)}, f32[96,3072]{1,0:T(8,128)}, f32[1,96]{1,0:T(1,128)}) custom-call(s32[4,4]{1,0:T(4,128)} %bitcast.13, bf16[1,768]{1,0:T(2,128)(2,1)} %gain_ref.1, bf16[8,64,768]{2,1,0:T(8,128)(2,1)} %bitcast.11, bf16[8,64,768]{2,1,0:T(8,128)(2,1)} %bitcast.12, bf16[768,3072]{1,0:T(8,128)(2,1)} %bitcast.9, bf16[768,3072]{1,0:T(8,128)(2,1)} %bitcast.10), custom_call_target="tpu_custom_call" | custom-call | flops 14495514624 | bytes 18874368 | tf_op jit(solution)/shard_map/window/pallas_call | solution.py:289
  133.7 0.0 copy-start
  133.7 2.5 %copy.12 = f32[1,96,3072]{2,1,0:T(8,128)} copy(f32[1,96,3072]{2,1,0:T(8,128)} %bitcast.8) | data formatting | bytes 2359296
  136.2 0.0 copy-done
  136.2 0.0 copy-start.1
  136.2 1.0 copy.13
  137.2 0.0 copy-done.1
  137.2 0.5 copy.14
Async XLA Ops:
  133.7 2.5 %copy-start = (f32[96,3072]{1,0:T(8,128)S(1)}, f32[96,3072]{1,0:T(8,128)}, u32[]{:S(2)}) copy-start(f32[96,3072]{1,0:T(8,128)} %get-tuple-element.7) | copy-start | bytes 3538948
  136.2 1.0 copy-start.1

commit v2 on v1

--- a/solution.py
+++ b/solution.py
@@ -13,9 +13,9 @@
 MESH = pl.DeviceIdType.MESH
 
 CHUNK_ROWS = 64
-LAG = 2
+LAG = 3
 HIDDEN_BLOCK = 512
-TILE = 512
+TILE = 256
 TRANSPOSED_RHS = (((1,), (1,)), ((), ()))
 
 
@@ -108,14 +108,54 @@
             branch += lax.dot_general(
                 active, w2[:, columns], TRANSPOSED_RHS, preferred_element_type=jnp.float32
             )
-
-        @pl.when(section < sections - 1)
+        h_out[index] = (inputs + keep_of(index) * branch).astype(jnp.bfloat16)
+        h_copy(index).start()
+
+        @pl.when(index == chunks - 1)
         def _():
-            h_out[index] = (inputs + keep_of(index) * branch).astype(jnp.bfloat16)
-            h_copy(index).start()
+            normed_t[...] = normed_all[...].T
+
+    def finish_chunk(index, inputs, inv_rms, upstream, grad_normed):
+        @pl.when(section > 0)
+        def _():
+            scaled = grad_normed * gain_row
+            centre = jnp.mean(scaled * inputs, axis=-1, keepdims=True)
+            grads = upstream + inv_rms * (scaled - inputs * inv_rms * inv_rms * centre)
+            g_out[index] = grads.astype(jnp.bfloat16)
+            g_copy(index).start()
+
+        gain_sum[0:1, :] += jnp.sum(grad_normed * inputs * inv_rms, axis=0, keepdims=True)
+
+    def both(index):
+        pl.when(section > 0)(lambda: h_copy(index).wait_recv())
+        rows = pl.ds(pl.multiple_of(index * chunk, chunk), chunk)
+        inputs = h_in[index].astype(jnp.float32)
+        inv_rms = lax.rsqrt(jnp.mean(inputs * inputs, axis=-1, keepdims=True) + EPSILON)
+        normed = (inputs * inv_rms * gain_row).astype(jnp.bfloat16)
+        normed_all[rows, :] = normed
+        upstream = g_in[index].astype(jnp.float32)
+        gated = (keep_of(index) * upstream).astype(jnp.bfloat16)
+        gated_all[rows, :] = gated
+        grad_normed = jnp.zeros((chunk, width), jnp.float32)
+        for columns in column_blocks:
+            hidden = jnp.dot(normed, w1[:, columns], preferred_element_type=jnp.float32)
+            grad_active = jnp.dot(gated, w2[:, columns], preferred_element_type=jnp.float32)
+            share = 0.5 * (1.0 + lax.erf(hidden * ROOT_HALF))
+            active_all[rows, columns] = (hidden * share).astype(jnp.bfloat16)
+            slope = share + hidden * jnp.exp(-0.5 * hidden * hidden) * DENSITY_SCALE
+            grad_hidden = (grad_active * slope).astype(jnp.bfloat16)
+            hidden_grad_all[rows, columns] = grad_hidden
+            grad_normed += lax.dot_general(
+                grad_hidden, w1[:, columns], TRANSPOSED_RHS, preferred_element_type=jnp.float32
+            )
+        finish_chunk(index, inputs, inv_rms, upstream, grad_normed)
+
+        @pl.when(index == chunks - 1)
+        def _():
+            normed_t[...] = normed_all[...].T
 
     def backward(index):
-        pl.when(section < sections - 1)(lambda: g_copy(index).wait_recv())
+        g_copy(index).wait_recv()
         rows = pl.ds(pl.multiple_of(index * chunk, chunk), chunk)
         inputs = h_in[index].astype(jnp.float32)
         inv_rms = lax.rsqrt(jnp.mean(inputs * inputs, axis=-1, keepdims=True) + EPSILON)
@@ -130,15 +170,7 @@
             grad_normed += lax.dot_general(
                 grad_hidden, w1[:, columns], TRANSPOSED_RHS, preferred_element_type=jnp.float32
             )
-        gain_sum[0:1, :] += jnp.sum(grad_normed * inputs * inv_rms, axis=0, keepdims=True)
-
-        @pl.when(section > 0)
-        def _():
-            scaled = grad_normed * gain_row
-            centre = jnp.mean(scaled * inputs, axis=-1, keepdims=True)
-            grads = upstream + inv_rms * (scaled - inputs * inv_rms * inv_rms * centre)
-            g_out[index] = grads.astype(jnp.bfloat16)
-            g_copy(index).start()
+        finish_chunk(index, inputs, inv_rms, upstream, grad_normed)
 
     pl.when(first)(entry.wait)
     for load in loads:
@@ -152,7 +184,17 @@
         pl.when(jnp.logical_and(behind >= 0, behind < chunks))(lambda: backward(behind))
         return carry
 
-    lax.fori_loop(0, chunks + 2 * LAG * (sections - 1), tick, 0)
+    def last_tick(index, carry):
+        both(index)
+        return carry
+
+    @pl.when(last)
+    def _():
+        lax.fori_loop(0, chunks, last_tick, 0)
+
+    @pl.when(section < sections - 1)
+    def _():
+        lax.fori_loop(0, chunks + 2 * LAG * (sections - 1), tick, 0)
 
     upwards = list(range(steps))
     downwards = upwards[:1] + upwards[:0:-1]
@@ -200,7 +242,6 @@
     fill_b, advance_b, close_b = halving(downwards, parts_b, landed_b, b_send, b_recv)
     fill_g, advance_g, close_g = halving(upwards, parts_g, landed_g, e_send, e_recv)
 
-    normed_t[...] = normed_all[...].T
     gated_t[...] = gated_all[...].T
     gain_lanes = jnp.broadcast_to(gain_sum[0:1, :], (128, width)).T
 

time: 138 us -> 128 us (0.928)
  Pallas kernels: 133 us -> 123 us
    pallas_call x1, Pallas kernels: 133 us -> 123 us  [per_device(): pl.pallas_call(functools.partial(kernel, dims), out_shape=(jax.ShapeDtype...]
where the time goes in v2:
time: 128 us
  Pallas kernels  123 us (96%)
  local copies, waits for them, and re-layouts  3.99 us (3%)
    pallas_call x1, Pallas kernels, per_device(): pl.pallas_call(functools.partial(kernel, dims), out_shape=(jax.ShapeDtype...  123 us
    unnamed x7, local copies, waits for them, and re-layouts  3.99 us

profile of v2, /device:TPU:0, one launch (start us, length us, event | category | flops | bytes accessed | tf_op | source)
XLA Modules:
  0.0 127.8 jit_solution(10631451430708146896)
XLA Ops:
  0.6 123.1 %window.1 = (f32[96,3072]{1,0:T(8,128)}, f32[96,3072]{1,0:T(8,128)}, f32[1,96]{1,0:T(1,128)}) custom-call(s32[4,4]{1,0:T(4,128)} %bitcast.13, bf16[1,768]{1,0:T(2,128)(2,1)} %gain_ref.1, bf16[8,64,768]{2,1,0:T(8,128)(2,1)} %bitcast.11, bf16[8,64,768]{2,1,0:T(8,128)(2,1)} %bitcast.12, bf16[768,3072]{1,0:T(8,128)(2,1)} %bitcast.9, bf16[768,3072]{1,0:T(8,128)(2,1)} %bitcast.10), custom_call_target="tpu_custom_call" | custom-call | flops 14495514624 | bytes 18874368 | tf_op jit(solution)/shard_map/window/pallas_call | solution.py:330
  123.8 0.0 copy-start
  123.8 2.5 %copy.12 = f32[1,96,3072]{2,1,0:T(8,128)} copy(f32[1,96,3072]{2,1,0:T(8,128)} %bitcast.8) | data formatting | bytes 2359296
  126.2 0.0 copy-done
  126.2 0.0 copy-start.1
  126.2 1.0 copy.13
  127.3 0.0 copy-done.1
  127.3 0.5 copy.14
Async XLA Ops:
  123.8 2.5 %copy-start = (f32[96,3072]{1,0:T(8,128)S(1)}, f32[96,3072]{1,0:T(8,128)}, u32[]{:S(2)}) copy-start(f32[96,3072]{1,0:T(8,128)} %get-tuple-element.7) | copy-start | bytes 3538948
  126.2 1.0 copy-start.1

commit v3 on v2

--- a/solution.py
+++ b/solution.py
@@ -37,11 +37,14 @@
 def kernel(
     dims, keep_ref, gain_ref, x_hbm, cot_hbm, w1_hbm, w2_hbm, grad_in_ref, grad_out_ref, grad_gain_ref,
     w1, w2, h_in, g_in, h_out, g_out, normed_all, gated_all, active_all, slope_all, hidden_grad_all,
-    gain_sum, normed_t, gated_t, parts_a, parts_b, parts_g, *rest,
+    gain_sum, normed_t, active_far, gated_far, own_t, far_t, parts_a, parts_b, parts_g, *rest,
 ):
     sections, shards, chunk, chunks, seq_len, block, tile, tiles, steps = dims
-    landed_a, landed_b, landed_g = rest[:steps], rest[steps : 2 * steps], rest[2 * steps : 3 * steps]
-    (load_sem, h_send, h_recv, g_send, g_recv, a_send, a_recv, b_send, b_recv, e_send, e_recv) = rest[3 * steps :]
+    landed_a = rest[:steps]
+    landed_b = rest[steps : 2 * steps - 1]
+    landed_g = rest[2 * steps - 1 : 3 * steps - 1]
+    (load_sem, h_send, h_recv, g_send, g_recv, a_send, a_recv, b_send, b_recv, e_send, e_recv,
+     active_send, active_recv, gated_send, gated_recv) = rest[3 * steps - 1 :]
     width, hidden_width = w1.shape
     section = lax.axis_index("section")
     shard = lax.axis_index("dp")
@@ -82,6 +85,26 @@
         return pltpu.make_async_remote_copy(
             g_out.at[index], g_in.at[index], g_send.at[index], g_recv.at[index],
             device_id={"section": section - 1}, device_id_type=MESH,
+        )
+
+    pair_bits = (1, steps - 1)
+    half_width = hidden_width // 2
+
+    def active_copy(index, half):
+        rows = pl.ds(pl.multiple_of(index * chunk, chunk), chunk)
+        columns = slice(half * half_width, (half + 1) * half_width)
+        return pltpu.make_async_remote_copy(
+            active_all.at[rows, columns], active_far.at[rows, columns],
+            active_send.at[index, half], active_recv.at[index, half],
+            device_id={"dp": partners[pair_bits[half]]}, device_id_type=MESH,
+        )
+
+    def gated_copy(index, half):
+        rows = pl.ds(pl.multiple_of(index * chunk, chunk), chunk)
+        return pltpu.make_async_remote_copy(
+            gated_all.at[rows], gated_far.at[half, rows],
+            gated_send.at[index, half], gated_recv.at[index, half],
+            device_id={"dp": partners[pair_bits[half]]}, device_id_type=MESH,
         )
 
     gain_row = gain_ref[...].astype(jnp.float32)
@@ -110,6 +133,8 @@
             )
         h_out[index] = (inputs + keep_of(index) * branch).astype(jnp.bfloat16)
         h_copy(index).start()
+        for half in range(2):
+            active_copy(index, half).start()
 
         @pl.when(index == chunks - 1)
         def _():
@@ -136,6 +161,8 @@
         upstream = g_in[index].astype(jnp.float32)
         gated = (keep_of(index) * upstream).astype(jnp.bfloat16)
         gated_all[rows, :] = gated
+        for half in range(2):
+            gated_copy(index, half).start()
         grad_normed = jnp.zeros((chunk, width), jnp.float32)
         for columns in column_blocks:
             hidden = jnp.dot(normed, w1[:, columns], preferred_element_type=jnp.float32)
@@ -148,6 +175,8 @@
             grad_normed += lax.dot_general(
                 grad_hidden, w1[:, columns], TRANSPOSED_RHS, preferred_element_type=jnp.float32
             )
+        for half in range(2):
+            active_copy(index, half).start()
         finish_chunk(index, inputs, inv_rms, upstream, grad_normed)
 
         @pl.when(index == chunks - 1)
@@ -162,6 +191,8 @@
         upstream = g_in[index].astype(jnp.float32)
         gated = (keep_of(index) * upstream).astype(jnp.bfloat16)
         gated_all[rows, :] = gated
+        for half in range(2):
+            gated_copy(index, half).start()
         grad_normed = jnp.zeros((chunk, width), jnp.float32)
         for columns in column_blocks:
             grad_active = jnp.dot(gated, w2[:, columns], preferred_element_type=jnp.float32)
@@ -196,13 +227,17 @@
     def _():
         lax.fori_loop(0, chunks + 2 * LAG * (sections - 1), tick, 0)
 
-    upwards = list(range(steps))
-    downwards = upwards[:1] + upwards[:0:-1]
+    orders_a = (list(range(steps)), [0] + list(range(steps - 1, 0, -1)))
+    orders_b = tuple(
+        [bit for bit in orders_a[1 - half] if bit != pair_bits[half]] for half in range(2)
+    )
     block_rows = width // shards
 
     def halving(order, parts, landed, send_sem, recv_sem):
+        count = 1 << len(order)
+
         def copy(at, step):
-            half = shards >> (step + 1)
+            half = count >> (step + 1)
             bit = order[step]
             source = parts if step == 0 else landed[step - 1]
             return pltpu.make_async_remote_copy(
@@ -214,84 +249,119 @@
                 device_id_type=MESH,
             )
 
-        def fill(at, value):
-            for shard_at in range(shards):
-                rows = value[shard_at * block_rows : (shard_at + 1) * block_rows]
-                parts[at, position(shard_at, order)] = rows.astype(jnp.bfloat16)
+        def fill(at, value, places):
+            for number, place in enumerate(places):
+                rows = value[number * block_rows : (number + 1) * block_rows]
+                parts[at, place] = rows.astype(jnp.bfloat16)
             copy(at, 0).start()
 
         def advance(at, step, finish):
             copy(at, step).wait_recv()
-            half = shards >> (step + 1)
+            half = count >> (step + 1)
             source = parts if step == 0 else landed[step - 1]
             own = source[at, pl.ds(bits[order[step]] * half, half)].astype(jnp.float32)
             total = own + landed[step][at].astype(jnp.float32)
-            if step + 1 < steps:
+            if step + 1 < len(order):
                 landed[step][at] = total.astype(jnp.bfloat16)
                 copy(at, step + 1).start()
             else:
                 finish(total[0])
 
         def close(at):
-            for step in range(steps):
+            for step in range(len(order)):
                 copy(at, step).wait_send()
 
         return fill, advance, close
 
-    fill_a, advance_a, close_a = halving(upwards, parts_a, landed_a, a_send, a_recv)
-    fill_b, advance_b, close_b = halving(downwards, parts_b, landed_b, b_send, b_recv)
-    fill_g, advance_g, close_g = halving(upwards, parts_g, landed_g, e_send, e_recv)
-
-    gated_t[...] = gated_all[...].T
+    streams_a = [halving(order, parts_a, landed_a, a_send, a_recv) for order in orders_a]
+    streams_b = [halving(order, parts_b, landed_b, b_send, b_recv) for order in orders_b]
+    fill_g, advance_g, close_g = halving(orders_a[0], parts_g, landed_g, e_send, e_recv)
     gain_lanes = jnp.broadcast_to(gain_sum[0:1, :], (128, width)).T
 
     def finish_gain(total):
         grad_gain_ref[...] = jnp.transpose(total)[0:1, :]
+
+    def select_features(ref, half, rows_first):
+        turned = rows_first.astype(jnp.float32).T
+        bit, order = pair_bits[half], orders_b[half]
+        for place in range(shards // 2):
+            low = sum(((place >> (len(order) - 1 - k)) & 1) << b for k, b in enumerate(order))
+            high = low + (1 << bit)
+            pieces = [turned[b * block_rows : (b + 1) * block_rows] for b in (low, high)]
+            chosen = jnp.where(bits[bit] == 1, pieces[1], pieces[0])
+            ref[half, place * block_rows : (place + 1) * block_rows] = chosen.astype(jnp.bfloat16)
+
+    def prepare_b():
+        def arrive(index, carry):
+            for half in range(2):
+                active_copy(index, half).wait_recv()
+                gated_copy(index, half).wait_recv()
+            return carry
+
+        lax.fori_loop(0, chunks, arrive, 0)
+        for half in range(2):
+            select_features(own_t, half, gated_all[...])
+            select_features(far_t, half, gated_far[half])
+
+    def columns_of(at, half):
+        return pl.ds(pl.multiple_of(at * tile + half * half_width, tile), tile)
 
     def turn(moment, carry):
         @pl.when(moment < tiles)
         def _():
-            columns = pl.ds(pl.multiple_of(moment * tile, tile), tile)
-            fill_a(
-                moment,
-                jnp.dot(normed_t[...], hidden_grad_all[:, columns], preferred_element_type=jnp.float32),
-            )
-            fill_b(
-                moment, jnp.dot(gated_t[...], active_all[:, columns], preferred_element_type=jnp.float32)
-            )
+            for half in range(2):
+                value = jnp.dot(
+                    normed_t[...],
+                    hidden_grad_all[:, columns_of(moment, half)],
+                    preferred_element_type=jnp.float32,
+                )
+                places = [position(b, orders_a[half]) for b in range(shards)]
+                streams_a[half][0](half * tiles + moment, value, places)
+            pl.when(moment == 0)(prepare_b)
+            for half in range(2):
+                columns = columns_of(moment, half)
+                value = jnp.dot(
+                    own_t[half], active_all[:, columns], preferred_element_type=jnp.float32
+                ) + jnp.dot(far_t[half], active_far[:, columns], preferred_element_type=jnp.float32)
+                streams_b[half][0](half * tiles + moment, value, range(shards // 2))
 
         for step in range(steps):
             at = moment - (step + 1)
 
             @pl.when(jnp.logical_and(at >= 0, at < tiles))
             def _(at=at, step=step):
-                columns = pl.ds(pl.multiple_of(at * tile, tile), tile)
-
-                def finish_a(total):
-                    grad_in_ref[:, columns] = total
-
-                def finish_b(total):
-                    grad_out_ref[:, columns] = total
-
-                advance_a(at, step, finish_a)
-                advance_b(at, step, finish_b)
+                def finish(out_ref, half):
+                    def store(total):
+                        out_ref[:, columns_of(at, half)] = total
+
+                    return store
+
+                for half in range(2):
+                    streams_a[half][1](half * tiles + at, step, finish(grad_in_ref, half))
+                if step + 1 < steps:
+                    for half in range(2):
+                        streams_b[half][1](half * tiles + at, step, finish(grad_out_ref, half))
 
             pl.when(moment == step + 2)(lambda step=step: advance_g(0, step, finish_gain))
         return carry
 
-    fill_g(0, gain_lanes)
+    fill_g(0, gain_lanes, [position(b, orders_a[0]) for b in range(shards)])
     lax.fori_loop(0, max(tiles, 2) + steps, turn, 0)
 
     def close_chunk(index, carry):
         pl.when(section < sections - 1)(lambda: h_copy(index).wait_send())
         pl.when(section > 0)(lambda: g_copy(index).wait_send())
+        for half in range(2):
+            active_copy(index, half).wait_send()
+            gated_copy(index, half).wait_send()
         return carry
 
     lax.fori_loop(0, chunks, close_chunk, 0)
 
     def close_tile(at, carry):
-        close_a(at)
-        close_b(at)
+        for half in range(2):
+            streams_a[half][2](half * tiles + at)
+            streams_b[half][2](half * tiles + at)
         return carry
 
     lax.fori_loop(0, tiles, close_tile, 0)
@@ -309,17 +379,17 @@
     chunk = largest_divisor(seq_len, CHUNK_ROWS, 16)
     chunks = rows // chunk
     block = largest_divisor(hidden_width, HIDDEN_BLOCK, 128)
-    tile = largest_divisor(hidden_width, TILE, 128)
-    tiles = hidden_width // tile
+    tile = largest_divisor(hidden_width // 2, TILE, 128)
+    tiles = hidden_width // 2 // tile
     steps = shards.bit_length() - 1
-    assert shards == 1 << steps and steps >= 1
+    assert shards == 1 << steps and steps >= 2
     block_rows = width // shards
     dims = (sections, shards, chunk, chunks, seq_len, block, tile, tiles, steps)
 
-    def landing(count, columns):
+    def landing(count, start, columns):
         return [
             pltpu.VMEM((count, shards >> (step + 1), block_rows, columns), jnp.bfloat16)
-            for step in range(steps)
+            for step in range(start, steps)
         ]
 
     chunk_shape = (chunks, chunk, width)
@@ -347,17 +417,21 @@
             pltpu.VMEM((rows, hidden_width), jnp.bfloat16),
             pltpu.VMEM((8, width), jnp.float32),
             pltpu.VMEM((width, rows), jnp.bfloat16),
-            pltpu.VMEM((width, rows), jnp.bfloat16),
-            pltpu.VMEM((tiles, shards, block_rows, tile), jnp.bfloat16),
-            pltpu.VMEM((tiles, shards, block_rows, tile), jnp.bfloat16),
+            pltpu.VMEM((rows, hidden_width), jnp.bfloat16),
+            pltpu.VMEM((2, rows, width), jnp.bfloat16),
+            pltpu.VMEM((2, width // 2, rows), jnp.bfloat16),
+            pltpu.VMEM((2, width // 2, rows), jnp.bfloat16),
+            pltpu.VMEM((2 * tiles, shards, block_rows, tile), jnp.bfloat16),
+            pltpu.VMEM((2 * tiles, shards // 2, block_rows, tile), jnp.bfloat16),
             pltpu.VMEM((1, shards, block_rows, 128), jnp.bfloat16),
-            *landing(tiles, tile),
-            *landing(tiles, tile),
-            *landing(1, 128),
+            *landing(2 * tiles, 0, tile),
+            *landing(2 * tiles, 1, tile),
+            *landing(1, 0, 128),
             dma((4,)),
             *[dma((chunks,)) for _ in range(4)],
-            *[dma((tiles, steps)) for _ in range(4)],
+            *[dma((2 * tiles, steps)) for _ in range(4)],
             *[dma((1, steps)) for _ in range(2)],
+            *[dma((chunks, 2)) for _ in range(4)],
         ],
         compiler_params=pltpu.CompilerParams(
             collective_id=0, has_side_effects=True, vmem_limit_bytes=62 * 1024 * 1024

time: 128 us -> 119 us (0.930)
  Pallas kernels: 123 us -> 114 us
    pallas_call x1, Pallas kernels: 123 us -> 114 us  [per_device(): pl.pallas_call(functools.partial(kernel, dims), out_shape=(jax.ShapeDtype...]
where the time goes in v3:
time: 119 us; the launch traced here: 118 us
  Pallas kernels  114 us (96%)
  local copies, waits for them, and re-layouts  3.99 us (3%)
    pallas_call x1, Pallas kernels, per_device(): pl.pallas_call(functools.partial(kernel, dims), out_shape=(jax.ShapeDtype...  114 us
    unnamed x7, local copies, waits for them, and re-layouts  3.99 us

profile of v3, /device:TPU:0, one launch (start us, length us, event | category | flops | bytes accessed | tf_op | source)
XLA Modules:
  0.0 118.4 jit_solution(12702745598425774515)
XLA Ops:
  0.6 113.8 %window.1 = (f32[96,3072]{1,0:T(8,128)}, f32[96,3072]{1,0:T(8,128)}, f32[1,96]{1,0:T(1,128)}) custom-call(s32[4,4]{1,0:T(4,128)} %bitcast.13, bf16[1,768]{1,0:T(2,128)(2,1)} %gain_ref.1, bf16[8,64,768]{2,1,0:T(8,128)(2,1)} %bitcast.11, bf16[8,64,768]{2,1,0:T(8,128)(2,1)} %bitcast.12, bf16[768,3072]{1,0:T(8,128)(2,1)} %bitcast.9, bf16[768,3072]{1,0:T(8,128)(2,1)} %bitcast.10), custom_call_target="tpu_custom_call" | custom-call | flops 14495514624 | bytes 18874368 | tf_op jit(solution)/shard_map/window/pallas_call | solution.py:400
  114.4 0.0 copy-start
  114.5 2.5 %copy.12 = f32[1,96,3072]{2,1,0:T(8,128)} copy(f32[1,96,3072]{2,1,0:T(8,128)} %bitcast.8) | data formatting | bytes 2359296
  116.9 0.0 copy-done
  116.9 0.0 copy-start.1
  116.9 1.0 copy.13
  117.9 0.0 copy-done.1
  117.9 0.5 copy.14
Async XLA Ops:
  114.4 2.5 %copy-start = (f32[96,3072]{1,0:T(8,128)S(1)}, f32[96,3072]{1,0:T(8,128)}, u32[]{:S(2)}) copy-start(f32[96,3072]{1,0:T(8,128)} %get-tuple-element.7) | copy-start | bytes 3538948
  116.9 1.0 copy-start.1

commit v4 on v3

--- a/solution.py
+++ b/solution.py
@@ -110,6 +110,49 @@
     gain_row = gain_ref[...].astype(jnp.float32)
     gain_sum[...] = jnp.zeros_like(gain_sum)
     column_blocks = [slice(at, at + block) for at in range(0, hidden_width, block)]
+
+    orders_a = (list(range(steps)), [0] + list(range(steps - 1, 0, -1)))
+    orders_b = tuple(
+        [bit for bit in orders_a[1 - half] if bit != pair_bits[half]] for half in range(2)
+    )
+    block_rows = width // shards
+    lots = 2 if chunks % 2 == 0 and chunks * chunk % 256 == 0 else 1
+    lot_rows = chunks * chunk // lots
+
+    def select_features(ref, half, turned, rows):
+        bit, order = pair_bits[half], orders_b[half]
+
+        def store(side):
+            for place in range(shards // 2):
+                at = sum(((place >> (len(order) - 1 - k)) & 1) << b for k, b in enumerate(order))
+                at = (at + (side << bit)) * block_rows
+                ref[half, place * block_rows : (place + 1) * block_rows, rows] = turned[
+                    at : at + block_rows
+                ].astype(jnp.bfloat16)
+
+        for side in range(2):
+            pl.when(bits[bit] == side)(lambda side=side: store(side))
+
+    def turned_rows(rows_first):
+        return (rows_first if block_rows % 16 == 0 else rows_first.astype(jnp.float32)).T
+
+    def prepare(lot):
+        def arrive(index, carry):
+            for half in range(2):
+                gated_copy(index, half).wait_recv()
+            return carry
+
+        lax.fori_loop(lot * (chunks // lots), (lot + 1) * (chunks // lots), arrive, 0)
+        rows = slice(lot * lot_rows, (lot + 1) * lot_rows)
+        turned = turned_rows(gated_all[rows, :])
+        for half in range(2):
+            select_features(own_t, half, turned, rows)
+        for half in range(2):
+            select_features(far_t, half, turned_rows(gated_far[half, rows]), rows)
+
+    def prepare_early():
+        for lot in range(lots - 1):
+            prepare(lot)
 
     def keep_of(index):
         return keep_ref[(index * chunk) // seq_len, section].astype(jnp.float32)
@@ -152,6 +195,7 @@
         gain_sum[0:1, :] += jnp.sum(grad_normed * inputs * inv_rms, axis=0, keepdims=True)
 
     def both(index):
+        pl.when(index == chunks - 1)(prepare_early)
         pl.when(section > 0)(lambda: h_copy(index).wait_recv())
         rows = pl.ds(pl.multiple_of(index * chunk, chunk), chunk)
         inputs = h_in[index].astype(jnp.float32)
@@ -159,10 +203,7 @@
         normed = (inputs * inv_rms * gain_row).astype(jnp.bfloat16)
         normed_all[rows, :] = normed
         upstream = g_in[index].astype(jnp.float32)
-        gated = (keep_of(index) * upstream).astype(jnp.bfloat16)
-        gated_all[rows, :] = gated
-        for half in range(2):
-            gated_copy(index, half).start()
+        gated = gated_all[rows, :]
         grad_normed = jnp.zeros((chunk, width), jnp.float32)
         for columns in column_blocks:
             hidden = jnp.dot(normed, w1[:, columns], preferred_element_type=jnp.float32)
@@ -184,6 +225,7 @@
             normed_t[...] = normed_all[...].T
 
     def backward(index):
+        pl.when(index == chunks - 1)(prepare_early)
         g_copy(index).wait_recv()
         rows = pl.ds(pl.multiple_of(index * chunk, chunk), chunk)
         inputs = h_in[index].astype(jnp.float32)
@@ -215,23 +257,25 @@
         pl.when(jnp.logical_and(behind >= 0, behind < chunks))(lambda: backward(behind))
         return carry
 
+    def send_gated(index, carry):
+        rows = pl.ds(pl.multiple_of(index * chunk, chunk), chunk)
+        gated_all[rows, :] = (keep_of(index) * g_in[index].astype(jnp.float32)).astype(jnp.bfloat16)
+        for half in range(2):
+            gated_copy(index, half).start()
+        return carry
+
     def last_tick(index, carry):
         both(index)
         return carry
 
     @pl.when(last)
     def _():
+        lax.fori_loop(0, chunks, send_gated, 0)
         lax.fori_loop(0, chunks, last_tick, 0)
 
     @pl.when(section < sections - 1)
     def _():
         lax.fori_loop(0, chunks + 2 * LAG * (sections - 1), tick, 0)
-
-    orders_a = (list(range(steps)), [0] + list(range(steps - 1, 0, -1)))
-    orders_b = tuple(
-        [bit for bit in orders_a[1 - half] if bit != pair_bits[half]] for half in range(2)
-    )
-    block_rows = width // shards
 
     def halving(order, parts, landed, send_sem, recv_sem):
         count = 1 << len(order)
@@ -276,38 +320,38 @@
     streams_a = [halving(order, parts_a, landed_a, a_send, a_recv) for order in orders_a]
     streams_b = [halving(order, parts_b, landed_b, b_send, b_recv) for order in orders_b]
     fill_g, advance_g, close_g = halving(orders_a[0], parts_g, landed_g, e_send, e_recv)
-    gain_lanes = jnp.broadcast_to(gain_sum[0:1, :], (128, width)).T
 
     def finish_gain(total):
         grad_gain_ref[...] = jnp.transpose(total)[0:1, :]
 
-    def select_features(ref, half, rows_first):
-        turned = rows_first.astype(jnp.float32).T
-        bit, order = pair_bits[half], orders_b[half]
-        for place in range(shards // 2):
-            low = sum(((place >> (len(order) - 1 - k)) & 1) << b for k, b in enumerate(order))
-            high = low + (1 << bit)
-            pieces = [turned[b * block_rows : (b + 1) * block_rows] for b in (low, high)]
-            chosen = jnp.where(bits[bit] == 1, pieces[1], pieces[0])
-            ref[half, place * block_rows : (place + 1) * block_rows] = chosen.astype(jnp.bfloat16)
-
-    def prepare_b():
-        def arrive(index, carry):
-            for half in range(2):
-                active_copy(index, half).wait_recv()
-                gated_copy(index, half).wait_recv()
-            return carry
-
-        lax.fori_loop(0, chunks, arrive, 0)
-        for half in range(2):
-            select_features(own_t, half, gated_all[...])
-            select_features(far_t, half, gated_far[half])
-
     def columns_of(at, half):
         return pl.ds(pl.multiple_of(at * tile + half * half_width, tile), tile)
 
+    def active_arrives(index, carry):
+        for half in range(2):
+            active_copy(index, half).wait_recv()
+        return carry
+
+    def finish(out_ref, at, half):
+        def store(total):
+            out_ref[:, columns_of(at, half)] = total
+
+        return store
+
+    def within(at):
+        return pl.when(jnp.logical_and(at >= 0, at < tiles))
+
+    def advance_all(streams, out_ref, at, step):
+        @within(at)
+        def _():
+            for half in range(2):
+                streams[half][1](half * tiles + at, step, finish(out_ref, at, half))
+
     def turn(moment, carry):
-        @pl.when(moment < tiles)
+        advance_all(streams_a, grad_in_ref, moment - 1, 0)
+        advance_all(streams_b, grad_out_ref, moment - 2, 0)
+
+        @within(moment)
         def _():
             for half in range(2):
                 value = jnp.dot(
@@ -317,35 +361,31 @@
                 )
                 places = [position(b, orders_a[half]) for b in range(shards)]
                 streams_a[half][0](half * tiles + moment, value, places)
-            pl.when(moment == 0)(prepare_b)
+
+        @pl.when(moment == 1)
+        def _():
+            prepare(lots - 1)
+            lax.fori_loop(0, chunks, active_arrives, 0)
+            gain_lanes = jnp.broadcast_to(gain_sum[0:1, :], (128, width)).T
+            fill_g(0, gain_lanes, [position(b, orders_a[0]) for b in range(shards)])
+
+        @within(moment - 1)
+        def _():
             for half in range(2):
-                columns = columns_of(moment, half)
+                columns = columns_of(moment - 1, half)
                 value = jnp.dot(
                     own_t[half], active_all[:, columns], preferred_element_type=jnp.float32
                 ) + jnp.dot(far_t[half], active_far[:, columns], preferred_element_type=jnp.float32)
-                streams_b[half][0](half * tiles + moment, value, range(shards // 2))
-
+                streams_b[half][0](half * tiles + moment - 1, value, range(shards // 2))
+
+        for step in range(1, steps):
+            advance_all(streams_a, grad_in_ref, moment - (step + 1), step)
+            if step + 1 < steps:
+                advance_all(streams_b, grad_out_ref, moment - (step + 2), step)
         for step in range(steps):
-            at = moment - (step + 1)
-
-            @pl.when(jnp.logical_and(at >= 0, at < tiles))
-            def _(at=at, step=step):
-                def finish(out_ref, half):
-                    def store(total):
-                        out_ref[:, columns_of(at, half)] = total
-
-                    return store
-
-                for half in range(2):
-                    streams_a[half][1](half * tiles + at, step, finish(grad_in_ref, half))
-                if step + 1 < steps:
-                    for half in range(2):
-                        streams_b[half][1](half * tiles + at, step, finish(grad_out_ref, half))
-
             pl.when(moment == step + 2)(lambda step=step: advance_g(0, step, finish_gain))
         return carry
 
-    fill_g(0, gain_lanes, [position(b, orders_a[0]) for b in range(shards)])
     lax.fori_loop(0, max(tiles, 2) + steps, turn, 0)
 
     def close_chunk(index, carry):

time: 119 us -> 122 us (1.025)
  Pallas kernels: 114 us -> 117 us
    pallas_call x1, Pallas kernels: 114 us -> 117 us  [per_device(): pl.pallas_call(functools.partial(kernel, dims), out_shape=(jax.ShapeDtype...]
where the time goes in v4:
time: 122 us
  Pallas kernels  117 us (96%)
  local copies, waits for them, and re-layouts  3.99 us (3%)
    pallas_call x1, Pallas kernels, per_device(): pl.pallas_call(functools.partial(kernel, dims), out_shape=(jax.ShapeDtype...  117 us
    unnamed x7, local copies, waits for them, and re-layouts  3.99 us

profile of v4, /device:TPU:0, one launch (start us, length us, event | category | flops | bytes accessed | tf_op | source)
XLA Modules:
  0.0 121.8 jit_solution(12551105722902331677)
XLA Ops:
  0.6 117.2 %window.1 = (f32[96,3072]{1,0:T(8,128)}, f32[96,3072]{1,0:T(8,128)}, f32[1,96]{1,0:T(1,128)}) custom-call(s32[4,4]{1,0:T(4,128)} %bitcast.13, bf16[1,768]{1,0:T(2,128)(2,1)} %gain_ref.1, bf16[8,64,768]{2,1,0:T(8,128)(2,1)} %bitcast.11, bf16[8,64,768]{2,1,0:T(8,128)(2,1)} %bitcast.12, bf16[768,3072]{1,0:T(8,128)(2,1)} %bitcast.9, bf16[768,3072]{1,0:T(8,128)(2,1)} %bitcast.10), custom_call_target="tpu_custom_call" | custom-call | flops 14495514624 | bytes 18874368 | tf_op jit(solution)/shard_map/window/pallas_call | solution.py:440
  117.8 0.0 copy-start
  117.8 2.5 %copy.12 = f32[1,96,3072]{2,1,0:T(8,128)} copy(f32[1,96,3072]{2,1,0:T(8,128)} %bitcast.8) | data formatting | bytes 2359296
  120.3 0.0 copy-done
  120.3 0.0 copy-start.1
  120.3 1.0 copy.13
  121.3 0.0 copy-done.1
  121.3 0.5 copy.14
Async XLA Ops:
  117.8 2.5 %copy-start = (f32[96,3072]{1,0:T(8,128)S(1)}, f32[96,3072]{1,0:T(8,128)}, u32[]{:S(2)}) copy-start(f32[96,3072]{1,0:T(8,128)} %get-tuple-element.7) | copy-start | bytes 3538948
  120.3 1.0 copy-start.1

commit v5 on v4

--- a/solution.py
+++ b/solution.py
@@ -195,7 +195,6 @@
         gain_sum[0:1, :] += jnp.sum(grad_normed * inputs * inv_rms, axis=0, keepdims=True)
 
     def both(index):
-        pl.when(index == chunks - 1)(prepare_early)
         pl.when(section > 0)(lambda: h_copy(index).wait_recv())
         rows = pl.ds(pl.multiple_of(index * chunk, chunk), chunk)
         inputs = h_in[index].astype(jnp.float32)
@@ -225,7 +224,7 @@
             normed_t[...] = normed_all[...].T
 
     def backward(index):
-        pl.when(index == chunks - 1)(prepare_early)
+        pl.when(index == chunks // 2 + 1)(prepare_early)
         g_copy(index).wait_recv()
         rows = pl.ds(pl.multiple_of(index * chunk, chunk), chunk)
         inputs = h_in[index].astype(jnp.float32)
@@ -271,6 +270,8 @@
     @pl.when(last)
     def _():
         lax.fori_loop(0, chunks, send_gated, 0)
+        for lot in range(lots):
+            prepare(lot)
         lax.fori_loop(0, chunks, last_tick, 0)
 
     @pl.when(section < sections - 1)
@@ -364,7 +365,7 @@
 
         @pl.when(moment == 1)
         def _():
-            prepare(lots - 1)
+            pl.when(section < sections - 1)(lambda: prepare(lots - 1))
             lax.fori_loop(0, chunks, active_arrives, 0)
             gain_lanes = jnp.broadcast_to(gain_sum[0:1, :], (128, width)).T
             fill_g(0, gain_lanes, [position(b, orders_a[0]) for b in range(shards)])

time: 122 us -> 128 us (1.049)
  Pallas kernels: 117 us -> 123 us
    pallas_call x1, Pallas kernels: 117 us -> 123 us  [per_device(): pl.pallas_call(functools.partial(kernel, dims), out_shape=(jax.ShapeDtype...]
where the time goes in v5:
time: 128 us
  Pallas kernels  123 us (96%)
  local copies, waits for them, and re-layouts  3.99 us (3%)
    pallas_call x1, Pallas kernels, per_device(): pl.pallas_call(functools.partial(kernel, dims), out_shape=(jax.ShapeDtype...  123 us
    unnamed x7, local copies, waits for them, and re-layouts  3.99 us

profile of v5, /device:TPU:0, one launch (start us, length us, event | category | flops | bytes accessed | tf_op | source)
XLA Modules:
  0.0 127.8 jit_solution(18374533202831338372)
XLA Ops:
  0.6 123.1 %window.1 = (f32[96,3072]{1,0:T(8,128)}, f32[96,3072]{1,0:T(8,128)}, f32[1,96]{1,0:T(1,128)}) custom-call(s32[4,4]{1,0:T(4,128)} %bitcast.13, bf16[1,768]{1,0:T(2,128)(2,1)} %gain_ref.1, bf16[8,64,768]{2,1,0:T(8,128)(2,1)} %bitcast.11, bf16[8,64,768]{2,1,0:T(8,128)(2,1)} %bitcast.12, bf16[768,3072]{1,0:T(8,128)(2,1)} %bitcast.9, bf16[768,3072]{1,0:T(8,128)(2,1)} %bitcast.10), custom_call_target="tpu_custom_call" | custom-call | flops 14495514624 | bytes 18874368 | tf_op jit(solution)/shard_map/window/pallas_call | solution.py:441
  123.8 0.0 copy-start
  123.8 2.5 %copy.12 = f32[1,96,3072]{2,1,0:T(8,128)} copy(f32[1,96,3072]{2,1,0:T(8,128)} %bitcast.8) | data formatting | bytes 2359296
  126.2 0.0 copy-done
  126.2 0.0 copy-start.1
  126.2 1.0 copy.13
  127.3 0.0 copy-done.1
  127.3 0.5 copy.14
Async XLA Ops:
  123.8 2.5 %copy-start = (f32[96,3072]{1,0:T(8,128)S(1)}, f32[96,3072]{1,0:T(8,128)}, u32[]{:S(2)}) copy-start(f32[96,3072]{1,0:T(8,128)} %get-tuple-element.7) | copy-start | bytes 3538948
  126.2 1.0 copy-start.1

commit v6 on v3

--- a/solution.py
+++ b/solution.py
@@ -159,10 +159,7 @@
         normed = (inputs * inv_rms * gain_row).astype(jnp.bfloat16)
         normed_all[rows, :] = normed
         upstream = g_in[index].astype(jnp.float32)
-        gated = (keep_of(index) * upstream).astype(jnp.bfloat16)
-        gated_all[rows, :] = gated
-        for half in range(2):
-            gated_copy(index, half).start()
+        gated = gated_all[rows, :]
         grad_normed = jnp.zeros((chunk, width), jnp.float32)
         for columns in column_blocks:
             hidden = jnp.dot(normed, w1[:, columns], preferred_element_type=jnp.float32)
@@ -215,12 +212,20 @@
         pl.when(jnp.logical_and(behind >= 0, behind < chunks))(lambda: backward(behind))
         return carry
 
+    def send_gated(index, carry):
+        rows = pl.ds(pl.multiple_of(index * chunk, chunk), chunk)
+        gated_all[rows, :] = (keep_of(index) * g_in[index].astype(jnp.float32)).astype(jnp.bfloat16)
+        for half in range(2):
+            gated_copy(index, half).start()
+        return carry
+
     def last_tick(index, carry):
         both(index)
         return carry
 
     @pl.when(last)
     def _():
+        lax.fori_loop(0, chunks, send_gated, 0)
         lax.fori_loop(0, chunks, last_tick, 0)
 
     @pl.when(section < sections - 1)
@@ -281,13 +286,12 @@
     def finish_gain(total):
         grad_gain_ref[...] = jnp.transpose(total)[0:1, :]
 
-    def select_features(ref, half, rows_first):
-        turned = rows_first.astype(jnp.float32).T
+    def select_features(ref, half, turned):
         bit, order = pair_bits[half], orders_b[half]
         for place in range(shards // 2):
             low = sum(((place >> (len(order) - 1 - k)) & 1) << b for k, b in enumerate(order))
             high = low + (1 << bit)
-            pieces = [turned[b * block_rows : (b + 1) * block_rows] for b in (low, high)]
+            pieces = [turned[b * block_rows : (b + 1) * block_rows].astype(jnp.float32) for b in (low, high)]
             chosen = jnp.where(bits[bit] == 1, pieces[1], pieces[0])
             ref[half, place * block_rows : (place + 1) * block_rows] = chosen.astype(jnp.bfloat16)
 
@@ -299,9 +303,14 @@
             return carry
 
         lax.fori_loop(0, chunks, arrive, 0)
-        for half in range(2):
-            select_features(own_t, half, gated_all[...])
-            select_features(far_t, half, gated_far[half])
+        def turn_rows(rows_first):
+            return (rows_first if block_rows % 16 == 0 else rows_first.astype(jnp.float32)).T
+
+        turned = turn_rows(gated_all[...])
+        for half in range(2):
+            select_features(own_t, half, turned)
+        for half in range(2):
+            select_features(far_t, half, turn_rows(gated_far[half]))
 
     def columns_of(at, half):
         return pl.ds(pl.multiple_of(at * tile + half * half_width, tile), tile)

time: 119 us -> 118 us (level)
  no operation moved by 1% of the time
where the time goes in v6:
time: 118 us
  Pallas kernels  114 us (97%)
  local copies, waits for them, and re-layouts  3.99 us (3%)
    pallas_call x1, Pallas kernels, per_device(): pl.pallas_call(functools.partial(kernel, dims), out_shape=(jax.ShapeDtype...  114 us
    unnamed x7, local copies, waits for them, and re-layouts  3.99 us

profile of v6, /device:TPU:0, one launch (start us, length us, event | category | flops | bytes accessed | tf_op | source)
XLA Modules:
  0.0 118.2 jit_solution(5522681655361584500)
XLA Ops:
  0.6 113.6 %window.1 = (f32[96,3072]{1,0:T(8,128)}, f32[96,3072]{1,0:T(8,128)}, f32[1,96]{1,0:T(1,128)}) custom-call(s32[4,4]{1,0:T(4,128)} %bitcast.13, bf16[1,768]{1,0:T(2,128)(2,1)} %gain_ref.1, bf16[8,64,768]{2,1,0:T(8,128)(2,1)} %bitcast.11, bf16[8,64,768]{2,1,0:T(8,128)(2,1)} %bitcast.12, bf16[768,3072]{1,0:T(8,128)(2,1)} %bitcast.9, bf16[768,3072]{1,0:T(8,128)(2,1)} %bitcast.10), custom_call_target="tpu_custom_call" | custom-call | flops 14495514624 | bytes 18874368 | tf_op jit(solution)/shard_map/window/pallas_call | solution.py:409
  114.2 0.0 copy-start
  114.2 2.5 %copy.12 = f32[1,96,3072]{2,1,0:T(8,128)} copy(f32[1,96,3072]{2,1,0:T(8,128)} %bitcast.8) | data formatting | bytes 2359296
  116.7 0.0 copy-done
  116.7 0.0 copy-start.1
  116.7 1.0 copy.13
  117.7 0.0 copy-done.1
  117.7 0.5 copy.14
Async XLA Ops:
  114.2 2.5 %copy-start = (f32[96,3072]{1,0:T(8,128)S(1)}, f32[96,3072]{1,0:T(8,128)}, u32[]{:S(2)}) copy-start(f32[96,3072]{1,0:T(8,128)} %get-tuple-element.7) | copy-start | bytes 3538948
  116.7 1.0 copy-start.1
